TPU v7x, 32 devices: a whole 2x2x4 slice. The times are simulated.
32 devices in a mesh: replica: 8 (over z, y), fsdp: 4 (over x, core).
Axes of the slice: x: 2, y: 2, z: 4, core: 2. Of those that a mesh axis runs over, the one named last changes fastest.
Arguments:
- tokens_in: bfloat16 [8, 1024, 1088], P('replica', 'fsdp'), may hold values from -6 to 6
- norm1_gain: bfloat16 [1088], P('fsdp'), may hold values from 0.099609375 to 1.8984375
- norm1_bias: bfloat16 [1088], P('fsdp'), may hold values from -3 to 3
- qkv_weight: bfloat16 [1088, 3264], P('fsdp'), may hold values from -0.1875 to 0.1875
- query_bias: bfloat16 [1088], P('fsdp'), may hold values from -3 to 3
- value_bias: bfloat16 [1088], P('fsdp'), may hold values from -3 to 3
- out_weight: bfloat16 [1088, 1088], P('fsdp'), may hold values from -1.5 to 1.5
- out_bias: bfloat16 [1088], P('fsdp'), may hold values from -3 to 3
- norm2_gain: bfloat16 [1088], P('fsdp'), may hold values from 0.099609375 to 1.8984375
- norm2_bias: bfloat16 [1088], P('fsdp'), may hold values from -3 to 3
- up_weight: bfloat16 [1088, 4352], P('fsdp'), may hold values from -0.1875 to 0.1875
- up_bias: bfloat16 [4352], P('fsdp'), may hold values from -3 to 3
- down_weight: bfloat16 [4352, 1088], P('fsdp'), may hold values from -0.09375 to 0.09375
- down_bias: bfloat16 [1088], P('fsdp'), may hold values from -3 to 3
- out_grad: bfloat16 [8, 1024, 1088], P('replica', 'fsdp'), may hold values from -6 to 6
Outputs:
- block_out: bfloat16 [8, 1024, 1088], P('replica', 'fsdp')
- input_grad: float32 [8, 1024, 1088], P('replica', 'fsdp')
- grad_norm1_gain: float32 [1088], P('fsdp')
- grad_norm1_bias: float32 [1088], P('fsdp')
- grad_qkv_weight: float32 [1088, 3264], P('fsdp')
- grad_query_bias: float32 [1088], P('fsdp')
- grad_value_bias: float32 [1088], P('fsdp')
- grad_out_weight: float32 [1088, 1088], P('fsdp')
- grad_out_bias: float32 [1088], P('fsdp')
- grad_norm2_gain: float32 [1088], P('fsdp')
- grad_norm2_bias: float32 [1088], P('fsdp')
- grad_up_weight: float32 [1088, 4352], P('fsdp')
- grad_up_bias: float32 [4352], P('fsdp')
- grad_down_weight: float32 [4352, 1088], P('fsdp')
- grad_down_bias: float32 [1088], P('fsdp')
All inputs are finite; a program needn't handle non-finite values.
Results may differ from a plain program's by a relative error of at most 0.019.
Values may be sent and summed in bfloat16 or wider, within the bound.
A program may use at most 256 MiB of HBM per device.

v0:
```python
import math

import jax
import jax.numpy as jnp
from jax import lax
from jax.sharding import PartitionSpec as P

HEADS = 17
HEAD_DIM = 64


EPSILON = 1e-05
MASKED = -1e30


def norm_rows(values, gain, shift):
    center = values - jnp.mean(values, axis=-1, keepdims=True)
    inverse = lax.rsqrt(jnp.mean(center * center, axis=-1, keepdims=True) + EPSILON)
    scaled = center * inverse
    return (scaled, inverse, scaled * gain + shift)


def norm_back(upstream, scaled, inverse, gain):
    weighted = upstream * gain
    inner = (
        weighted
        - jnp.mean(weighted, axis=-1, keepdims=True)
        - scaled * jnp.mean(weighted * scaled, axis=-1, keepdims=True)
    )
    return (inverse * inner, jnp.sum(upstream * scaled, axis=0), jnp.sum(upstream, axis=0))


def gelu_exact(values):
    return 0.5 * values * (1.0 + jax.scipy.special.erf(values * (1.0 / math.sqrt(2.0))))


def masked_scores(row_heads, key_heads, row_index, key_index, factor):
    raw_scores = jnp.einsum(
        "sqhe,skhe->shqk", row_heads, key_heads, preferred_element_type=jnp.float32
    )
    allowed = key_index[None, :] <= row_index[:, None]
    return jnp.where(allowed[None, None], raw_scores * factor, MASKED)


def pair_terms(
    row_heads,
    grad_heads,
    key_heads,
    value_heads,
    row_index,
    key_index,
    log_total,
    delta_rows,
    factor,
):
    scores = masked_scores(row_heads, key_heads, row_index, key_index, factor)
    probs_full = jnp.exp(scores - log_total[..., None])
    prob_grads = jnp.einsum(
        "sqhe,skhe->shqk", grad_heads, value_heads, preferred_element_type=jnp.float32
    )
    score_grads = (probs_full * (prob_grads - delta_rows[..., None])).astype(jnp.bfloat16)
    return (probs_full.astype(jnp.bfloat16), score_grads)


def shards(
    tokens_in,
    norm1_gain,
    norm1_bias,
    qkv_weight,
    query_bias,
    value_bias,
    out_weight,
    out_bias,
    norm2_gain,
    norm2_bias,
    up_weight,
    up_bias,
    down_weight,
    down_bias,
    out_grad,
):
    owned_shards = (
        norm1_gain,
        norm1_bias,
        qkv_weight,
        query_bias,
        value_bias,
        out_weight,
        out_bias,
        norm2_gain,
        norm2_bias,
        up_weight,
        up_bias,
        down_weight,
        down_bias,
    )
    gathered = (
        lax.all_gather(owned_shards[0], "fsdp", axis=0, tiled=True),
        lax.all_gather(owned_shards[1], "fsdp", axis=0, tiled=True),
        lax.all_gather(owned_shards[2], "fsdp", axis=0, tiled=True),
        lax.all_gather(owned_shards[3], "fsdp", axis=0, tiled=True),
        lax.all_gather(owned_shards[4], "fsdp", axis=0, tiled=True),
        lax.all_gather(owned_shards[5], "fsdp", axis=0, tiled=True),
        lax.all_gather(owned_shards[6], "fsdp", axis=0, tiled=True),
        lax.all_gather(owned_shards[7], "fsdp", axis=0, tiled=True),
        lax.all_gather(owned_shards[8], "fsdp", axis=0, tiled=True),
        lax.all_gather(owned_shards[9], "fsdp", axis=0, tiled=True),
        lax.all_gather(owned_shards[10], "fsdp", axis=0, tiled=True),
        lax.all_gather(owned_shards[11], "fsdp", axis=0, tiled=True),
        lax.all_gather(owned_shards[12], "fsdp", axis=0, tiled=True),
    )
    (
        first_gain,
        first_shift,
        full_qkv,
        query_shift,
        value_shift,
        full_out,
        out_shift,
        second_gain,
        second_shift,
        full_up,
        up_shift,
        full_down,
        down_shift,
    ) = gathered
    sequences, local_len, model_width = tokens_in.shape
    row_count = sequences * local_len
    device_index = lax.axis_index("fsdp")
    factor = 1.0 / math.sqrt(HEAD_DIM)
    inputs = tokens_in.astype(jnp.float32).reshape(row_count, model_width)
    scaled_one, inverse_one, normed_one = norm_rows(
        inputs, first_gain.astype(jnp.float32), first_shift.astype(jnp.float32)
    )
    normed_low = normed_one.astype(jnp.bfloat16)
    projected = jnp.dot(normed_low, full_qkv, preferred_element_type=jnp.float32)
    queries = (projected[:, :model_width] + query_shift.astype(jnp.float32)).astype(jnp.bfloat16)
    key_rows = projected[:, model_width : 2 * model_width].astype(jnp.bfloat16)
    value_rows = (projected[:, 2 * model_width :] + value_shift.astype(jnp.float32)).astype(
        jnp.bfloat16
    )
    key_all, value_all = (
        lax.all_gather(
            key_rows.reshape(sequences, local_len, model_width), "fsdp", axis=1, tiled=True
        ),
        lax.all_gather(
            value_rows.reshape(sequences, local_len, model_width), "fsdp", axis=1, tiled=True
        ),
    )
    full_len = key_all.shape[1]
    key_block = min(512, full_len)
    key_turns = full_len // key_block
    query_heads = queries.reshape(sequences, local_len, HEADS, HEAD_DIM)
    row_index = device_index * local_len + jnp.arange(local_len, dtype=jnp.int32)
    block_range = jnp.arange(key_block, dtype=jnp.int32)

    def key_slices(offset):
        key_heads = lax.dynamic_slice_in_dim(key_all, offset, key_block, 1).reshape(
            sequences, key_block, HEADS, HEAD_DIM
        )
        value_heads = lax.dynamic_slice_in_dim(value_all, offset, key_block, 1).reshape(
            sequences, key_block, HEADS, HEAD_DIM
        )
        return (key_heads, value_heads)

    def forward_step(block_index, running):
        highest, row_total, summed = running
        offset = block_index * key_block
        key_heads, value_heads = key_slices(offset)
        scores = masked_scores(query_heads, key_heads, row_index, offset + block_range, factor)
        new_high = jnp.maximum(highest, jnp.max(scores, axis=-1))
        fading = jnp.exp(highest - new_high)
        weights = jnp.exp(scores - new_high[..., None])
        row_total = row_total * fading + jnp.sum(weights, axis=-1)
        summed = summed * fading[..., None] + jnp.einsum(
            "shqk,skhe->shqe",
            weights.astype(jnp.bfloat16),
            value_heads,
            preferred_element_type=jnp.float32,
        )
        return (new_high, row_total, summed)

    start_state = (
        jnp.full((sequences, HEADS, local_len), MASKED, jnp.float32),
        jnp.zeros((sequences, HEADS, local_len), jnp.float32),
        jnp.zeros((sequences, HEADS, local_len, HEAD_DIM), jnp.float32),
    )
    highest, row_total, summed = lax.fori_loop(0, key_turns, forward_step, start_state)
    log_total = highest + jnp.log(row_total)
    attended = jnp.transpose(summed / row_total[..., None], (0, 2, 1, 3))
    attended_low = attended.reshape(row_count, model_width).astype(jnp.bfloat16)
    middle = (
        inputs
        + jnp.dot(attended_low, full_out, preferred_element_type=jnp.float32)
        + out_shift.astype(jnp.float32)
    )
    scaled_two, inverse_two, normed_two = norm_rows(
        middle, second_gain.astype(jnp.float32), second_shift.astype(jnp.float32)
    )
    second_low = normed_two.astype(jnp.bfloat16)
    pre_act = jnp.dot(second_low, full_up, preferred_element_type=jnp.float32) + up_shift.astype(
        jnp.float32
    )
    hidden_full, gelu_pull = jax.vjp(gelu_exact, pre_act)
    hidden = hidden_full.astype(jnp.bfloat16)
    result = (
        middle
        + jnp.dot(hidden, full_down, preferred_element_type=jnp.float32)
        + down_shift.astype(jnp.float32)
    )
    block_out = result.astype(jnp.bfloat16).reshape(sequences, local_len, model_width)
    back_gain_one, back_qkv, back_out = (first_gain, full_qkv, full_out)
    back_gain_two, back_up, back_down = (second_gain, full_up, full_down)
    upstream = out_grad.reshape(row_count, model_width)
    upstream_full = upstream.astype(jnp.float32)
    grad_down = jnp.einsum("rf,rd->fd", hidden, upstream, preferred_element_type=jnp.float32)
    grad_down_shift = jnp.sum(upstream_full, axis=0)
    hidden_grad = jnp.einsum("rd,fd->rf", upstream, back_down, preferred_element_type=jnp.float32)
    pre_grad = gelu_pull(hidden_grad)[0].astype(jnp.bfloat16)
    grad_up = jnp.einsum("rd,rf->df", second_low, pre_grad, preferred_element_type=jnp.float32)
    grad_up_shift = jnp.sum(pre_grad.astype(jnp.float32), axis=0)
    second_grad = jnp.einsum("rf,df->rd", pre_grad, back_up, preferred_element_type=jnp.float32)
    middle_norm_grad, grad_second_gain, grad_second_shift = norm_back(
        second_grad, scaled_two, inverse_two, back_gain_two.astype(jnp.float32)
    )
    middle_grad = upstream_full + middle_norm_grad
    middle_low = middle_grad.astype(jnp.bfloat16)
    grad_out = jnp.einsum("re,rd->ed", attended_low, middle_low, preferred_element_type=jnp.float32)
    grad_out_shift = jnp.sum(middle_low.astype(jnp.float32), axis=0)
    attended_grad = jnp.einsum(
        "rd,ed->re", middle_low, back_out, preferred_element_type=jnp.float32
    ).astype(jnp.bfloat16)
    grad_heads = attended_grad.reshape(sequences, local_len, HEADS, HEAD_DIM)
    delta_rows = jnp.transpose(
        jnp.sum(grad_heads.astype(jnp.float32) * attended, axis=-1), (0, 2, 1)
    )
    query_start = jnp.zeros((sequences, local_len, HEADS, HEAD_DIM), jnp.float32)

    def backward_step(block_index, running):
        query_grad, key_grads, value_grads = running
        offset = block_index * key_block
        key_heads, value_heads = key_slices(offset)
        probs_low, score_grads = pair_terms(
            query_heads,
            grad_heads,
            key_heads,
            value_heads,
            row_index,
            offset + block_range,
            log_total,
            delta_rows,
            factor,
        )
        query_grad = (
            query_grad
            + jnp.einsum(
                "shqk,skhe->sqhe", score_grads, key_heads, preferred_element_type=jnp.float32
            )
            * factor
        )
        key_part = (
            jnp.einsum(
                "shqk,sqhe->skhe", score_grads, query_heads, preferred_element_type=jnp.float32
            )
            * factor
        )
        value_part = jnp.einsum(
            "shqk,sqhe->skhe", probs_low, grad_heads, preferred_element_type=jnp.float32
        )
        key_grads = lax.dynamic_update_slice_in_dim(
            key_grads, key_part.reshape(sequences, key_block, model_width), offset, 1
        )
        value_grads = lax.dynamic_update_slice_in_dim(
            value_grads, value_part.reshape(sequences, key_block, model_width), offset, 1
        )
        return (query_grad, key_grads, value_grads)

    start_back = (
        query_start,
        jnp.zeros((sequences, full_len, model_width), jnp.float32),
        jnp.zeros((sequences, full_len, model_width), jnp.float32),
    )
    query_grad, key_grads, value_grads = lax.fori_loop(0, key_turns, backward_step, start_back)
    own_key_grad, own_value_grad = (
        lax.psum_scatter(
            key_grads.astype(jnp.bfloat16), "fsdp", scatter_dimension=1, tiled=True
        ).astype(jnp.float32),
        lax.psum_scatter(
            value_grads.astype(jnp.bfloat16), "fsdp", scatter_dimension=1, tiled=True
        ).astype(jnp.float32),
    )
    qkv_grad = jnp.concatenate(
        [
            query_grad.reshape(row_count, model_width),
            own_key_grad.reshape(row_count, model_width),
            own_value_grad.reshape(row_count, model_width),
        ],
        axis=1,
    ).astype(jnp.bfloat16)
    grad_qkv = jnp.einsum("rd,rc->dc", normed_low, qkv_grad, preferred_element_type=jnp.float32)
    grad_query_shift = jnp.sum(qkv_grad[:, :model_width].astype(jnp.float32), axis=0)
    grad_value_shift = jnp.sum(qkv_grad[:, 2 * model_width :].astype(jnp.float32), axis=0)
    first_grad = jnp.einsum("rc,dc->rd", qkv_grad, back_qkv, preferred_element_type=jnp.float32)
    input_norm_grad, grad_first_gain, grad_first_shift = norm_back(
        first_grad, scaled_one, inverse_one, back_gain_one.astype(jnp.float32)
    )
    input_grad = (middle_grad + input_norm_grad).reshape(sequences, local_len, model_width)
    local_grads = (
        grad_first_gain,
        grad_first_shift,
        grad_qkv,
        grad_query_shift,
        grad_value_shift,
        grad_out,
        grad_out_shift,
        grad_second_gain,
        grad_second_shift,
        grad_up,
        grad_up_shift,
        grad_down,
        grad_down_shift,
    )
    owned = (
        lax.psum_scatter(
            local_grads[0].astype(jnp.bfloat16), "fsdp", scatter_dimension=0, tiled=True
        ).astype(jnp.float32),
        lax.psum_scatter(
            local_grads[1].astype(jnp.bfloat16), "fsdp", scatter_dimension=0, tiled=True
        ).astype(jnp.float32),
        lax.psum_scatter(
            local_grads[2].astype(jnp.bfloat16), "fsdp", scatter_dimension=0, tiled=True
        ).astype(jnp.float32),
        lax.psum_scatter(
            local_grads[3].astype(jnp.bfloat16), "fsdp", scatter_dimension=0, tiled=True
        ).astype(jnp.float32),
        lax.psum_scatter(
            local_grads[4].astype(jnp.bfloat16), "fsdp", scatter_dimension=0, tiled=True
        ).astype(jnp.float32),
        lax.psum_scatter(
            local_grads[5].astype(jnp.bfloat16), "fsdp", scatter_dimension=0, tiled=True
        ).astype(jnp.float32),
        lax.psum_scatter(
            local_grads[6].astype(jnp.bfloat16), "fsdp", scatter_dimension=0, tiled=True
        ).astype(jnp.float32),
        lax.psum_scatter(
            local_grads[7].astype(jnp.bfloat16), "fsdp", scatter_dimension=0, tiled=True
        ).astype(jnp.float32),
        lax.psum_scatter(
            local_grads[8].astype(jnp.bfloat16), "fsdp", scatter_dimension=0, tiled=True
        ).astype(jnp.float32),
        lax.psum_scatter(
            local_grads[9].astype(jnp.bfloat16), "fsdp", scatter_dimension=0, tiled=True
        ).astype(jnp.float32),
        lax.psum_scatter(
            local_grads[10].astype(jnp.bfloat16), "fsdp", scatter_dimension=0, tiled=True
        ).astype(jnp.float32),
        lax.psum_scatter(
            local_grads[11].astype(jnp.bfloat16), "fsdp", scatter_dimension=0, tiled=True
        ).astype(jnp.float32),
        lax.psum_scatter(
            local_grads[12].astype(jnp.bfloat16), "fsdp", scatter_dimension=0, tiled=True
        ).astype(jnp.float32),
    )
    flattened = jnp.concatenate([member.reshape(-1) for member in owned])
    share = lax.psum_scatter(
        flattened.astype(jnp.bfloat16), "replica", scatter_dimension=0, tiled=True
    ).astype(jnp.float32)
    summed_all = lax.all_gather(share.astype(jnp.bfloat16), "replica", axis=0, tiled=True).astype(
        share.dtype
    )
    totals = []
    position = 0
    for member in owned:
        length_of = member.size
        totals.append(summed_all[position : position + length_of].reshape(member.shape))
        position = position + length_of
    return (
        block_out,
        input_grad,
        totals[0],
        totals[1],
        totals[2],
        totals[3],
        totals[4],
        totals[5],
        totals[6],
        totals[7],
        totals[8],
        totals[9],
        totals[10],
        totals[11],
        totals[12],
    )


def solution(mesh):
    placed = (
        P("replica", "fsdp", None),
        P("fsdp"),
        P("fsdp"),
        P("fsdp", None),
        P("fsdp"),
        P("fsdp"),
        P("fsdp", None),
        P("fsdp"),
        P("fsdp"),
        P("fsdp"),
        P("fsdp", None),
        P("fsdp"),
        P("fsdp", None),
        P("fsdp"),
        P("replica", "fsdp", None),
    )
    return jax.shard_map(
        shards,
        mesh=mesh,
        in_specs=placed,
        out_specs=(
            P("replica", "fsdp", None),
            P("replica", "fsdp", None),
            P("fsdp"),
            P("fsdp"),
            P("fsdp", None),
            P("fsdp"),
            P("fsdp"),
            P("fsdp", None),
            P("fsdp"),
            P("fsdp"),
            P("fsdp"),
            P("fsdp", None),
            P("fsdp"),
            P("fsdp", None),
            P("fsdp"),
        ),
        check_vma=False,
    )
```

profile of v0, /device:TPU:0, one launch (start us, length us, event | category | flops | bytes accessed | tf_op | source)
XLA Modules:
  0.0 1338.9 jit_solution(6080002411256555360)
XLA Ops:
  17.6 14.3 %all-reduce.21 = (bf16[1088]{0:T(1024)(128)(2,1)S(1)}, bf16[1088]{0:T(1024)(128)(2,1)S(1)}, bf16[1088]{0:T(1024)(128)(2,1)S(1)}, bf16[1088]{0:T(1024)(128)(2,1)S...) all-reduce(bf16[1088]{0:T(1024)(128)(2,1)S(1)} %dynamic-update-slic, ...), channel_id=1, replica_groups=mesh['replica'=8,'fsdp'=4] {'fsdp'}, use_global_device_ids=true, to_apply=%add.1 | all-reduce | flops 11968 | bytes 47872
  32.4 32.3 %all-gather.9.cloned.1.call-done = bf16[1088,3264]{1,0:T(8,128)(2,1)} async-done(((bf16[272,3264]{1,0:T(8,128)(2,1)}), bf16[1088,3264]{1,0:T(8,128)(2,1)}) %all-gather.9.cloned.1.call-update) | async-done | bytes 7102480 | tf_op jit(solution)/shard_map/all_gather | solution.py:100
  64.8 6.7 fusion.78
  79.0 19.0 %all-gather.17.cloned.1.call-done = bf16[1024,1088]{0,1:T(8,128)(2,1)} async-done(((bf16[256,1088]{0,1:T(8,128)(2,1)}), bf16[1024,1088]{0,1:T(8,128)(2,1)}) %all-gather.17.cloned.1.call-update) | async-done | bytes 2228240 | tf_op jit(solution)/shard_map/all_gather | solution.py:143
  98.0 25.8 %all-gather.19.cloned.1.call-done = bf16[1024,1088]{0,1:T(8,128)(2,1)} async-done(((bf16[256,1088]{0,1:T(8,128)(2,1)}), bf16[1024,1088]{0,1:T(8,128)(2,1)}) %all-gather.19.cloned.1.call-update) | async-done | bytes 2228240 | tf_op jit(solution)/shard_map/all_gather | solution.py:146
  123.8 38.5 %while.36 = (s32[]{:T(128)}, f32[1,17,256]{2,1,0:T(8,128)S(1)}, f32[1,17,256]{2,1,0:T(8,128)S(1)}, f32[1,17,256,64]{2,3,1,0:T(8,128)}, bf16[1,1024,1088]{1,2,0:T...) while((s32[]{:T(128)}, f32[1,17,256]{2,1,0:T(8,128)S(1)}, ...), condition=%wide.region_5.6_spmd.clone, body=%wide.region_2.5_spmd.clone.sunk | while | flops 595929344 | bytes 72669408 | solution.py:188
  131.8 6.0 fusion.134
  168.2 47.8 %all-gather.13.cloned.1.call-done = bf16[1088,4352]{1,0:T(8,128)(2,1)} async-done(((bf16[272,4352]{1,0:T(8,128)(2,1)}), bf16[1088,4352]{1,0:T(8,128)(2,1)}) %all-gather.13.cloned.1.call-update) | async-done | bytes 9469968 | tf_op jit(solution)/shard_map/all_gather | solution.py:107
  216.0 8.2 multiply_convert_fusion
  224.2 60.8 %all-gather.15.cloned.1.call-done = bf16[4352,1088]{1,0:T(8,128)(2,1)} async-done(((bf16[1088,1088]{1,0:T(8,128)(2,1)}), bf16[4352,1088]{1,0:T(8,128)(2,1)}) %all-gather.15.cloned.1.call-update) | async-done | bytes 9469968 | tf_op jit(solution)/shard_map/all_gather | solution.py:109
  285.0 7.7 fusion.86
  302.7 46.2 %while.37 = (s32[]{:T(128)}, f32[1,256,17,64]{1,3,2,0:T(8,128)S(1)}, bf16[1,1024,1088]{1,2,0:T(8,128)(2,1)}, bf16[1,1024,1088]{1,2,0:T(8,128)(2,1)}, bf16[1,1024...) while((s32[]{:T(128)}, ...), condition=%wide.region_12.13_spmd.clone, body=%wide.region_11.12_spmd.clone.sunk | while | flops 1450427136 | bytes 157541904 | solution.py:283
  306.0 5.9 fusion.147
  315.2 5.8 fusion.149
  329.1 5.9 fusion.147
  353.2 28.1 %reduce-scatter.9.cloned.1.call-done = bf16[1,256,1088]{1,2,0:T(8,128)(2,1)} async-done(((bf16[1,1024,1088]{1,2,0:T(8,128)(2,1)}), bf16[1,256,1088]{1,2,0:T(8,128)(2,1)}) %reduce-scatter.9.cloned.1.call-update) | async-done | bytes 557072 | tf_op jit(solution)/shard_map/reduce_scatter | solution.py:288
  381.3 35.0 %reduce-scatter.7.cloned.1.call-done = bf16[1,256,1088]{1,2,0:T(8,128)(2,1)} async-done(((bf16[1,1024,1088]{1,2,0:T(8,128)(2,1)}), bf16[1,256,1088]{1,2,0:T(8,128)(2,1)}) %reduce-scatter.7.cloned.1.call-update) | async-done | bytes 557072 | tf_op jit(solution)/shard_map/reduce_scatter | solution.py:285
  416.4 5.8 convolution_convert_fusion.2
  431.3 6.6 convolution_convert_fusion
  442.3 6.9 fusion.62
  449.1 10.7 all-reduce.20
  463.3 57.7 %reduce-scatter.11.cloned.1.call-done = bf16[272,3264]{1,0:T(8,128)(2,1)} async-done(((bf16[1088,3264]{1,0:T(8,128)(2,1)}), bf16[272,3264]{1,0:T(8,128)(2,1)}) %reduce-scatter.11.cloned.1.call-update) | async-done | bytes 1775632 | tf_op jit(solution)/shard_map/reduce_scatter | solution.py:330
  525.4 76.8 %reduce-scatter.15.cloned.1.call-done = bf16[272,4352]{1,0:T(8,128)(2,1)} async-done(((bf16[1088,4352]{1,0:T(8,128)(2,1)}), bf16[272,4352]{1,0:T(8,128)(2,1)}) %reduce-scatter.15.cloned.1.call-update) | async-done | bytes 2367504 | tf_op jit(solution)/shard_map/reduce_scatter | solution.py:351
  607.8 79.2 %reduce-scatter.17.cloned.1.call-done = bf16[1088,1088]{1,0:T(8,128)(2,1)} async-done(((bf16[4352,1088]{1,0:T(8,128)(2,1)}), bf16[1088,1088]{1,0:T(8,128)(2,1)}) %reduce-scatter.17.cloned.1.call-update) | async-done | bytes 2367504 | tf_op jit(solution)/shard_map/reduce_scatter | solution.py:357
  687.0 6.0 reshape.396
  693.0 118.0 %concatenate.9 = bf16[3554496]{0:T(1024)(128)(2,1)} concatenate(bf16[272]{0:T(512)(128)(2,1)S(1)} %dynamic-slice.11, bf16[272]{0:T(512)(128)(2,1)S(1)} %dynamic-slice.13, bf16[887808]{0:T(1024)(128)(2,1)} %reshape.393, bf16[272]{0:T(512)(128)(2,1)S(1)} %dynamic-slice.15, bf16[272]{0:T(512)(128)(2,1)S(1)} %dynamic-slice.17, bf16[295936]{0:T(1024)(128)(2,1)} %reshape.394, ...), dimensions={0} | concatenate | bytes 14217984 | tf_op jit(solution)/shard_map/concatenate | solution.py:364
  812.6 234.4 %all-reduce.27.cloned.1.call-done = bf16[3554496]{0:T(1024)(128)(2,1)} async-done(((bf16[3554496]{0:T(1024)(128)(2,1)}), bf16[3554496]{0:T(1024)(128)(2,1)}) %all-reduce.27.cloned.1.call-update) | async-done | bytes 7109008
  1052.9 14.8 %dynamic-update-slice.9 = bf16[3554496]{0:T(1024)(128)(2,1)} dynamic-update-slice(bf16[3554496]{0:T(1024)(128)(2,1)} %broadcast.225, bf16[444312]{0:T(1024)(128)(2,1)} %dynamic-slice.29, u32[]{:T(128)} %bitcast.18) | dynamic-update-slice | bytes 1777252
  1070.8 9.4 fusion.47
  1080.2 222.6 %all-reduce.25.cloned.1.call-done = bf16[3554496]{0:T(1024)(128)(2,1)} async-done(((bf16[3554496]{0:T(1024)(128)(2,1)}), bf16[3554496]{0:T(1024)(128)(2,1)}) %all-reduce.25.cloned.1.call-update) | async-done | bytes 7109008
  1310.8 6.4 fusion.82
  1322.9 6.3 reshape.399
  (246 shorter events, 149.0 us)
Async XLA Ops:
  7.2 24.8 %copy-start.14 = (bf16[1,256,1088]{1,2,0:T(8,128)(2,1)S(1)}, bf16[1,256,1088]{1,2,0:T(8,128)(2,1)}, u32[]{:S(2)}) copy-start(bf16[1,256,1088]{1,2,0:T(8,128)(2,1)} %param.19) | copy-start | bytes 1671172
  7.2 57.6 %all-gather.9.cloned.1.call-start = ((), (), s32[]{:S(2)}) async-start(), calls=%async_computation.6 | async-start | bytes 9052160 | tf_op jit(solution)/shard_map/all_gather | solution.py:100
  7.9 90.1 %all-gather.17.cloned.1.call-start = ((), (), s32[]{:S(2)}) async-start(), calls=%async_computation.16 | async-start | bytes 2785280 | tf_op jit(solution)/shard_map/all_gather | solution.py:143
  32.0 39.5 %copy-start.28 = (f32[1088]{0:T(1024)}, f32[1088]{0:T(1024)S(1)}, u32[]{:S(2)}) copy-start(f32[1088]{0:T(1024)S(1)} %convert_element_type.167) | copy-start | bytes 13060
  32.0 39.5 %copy-start.24 = (f32[1088]{0:T(1024)}, f32[1088]{0:T(1024)S(1)}, u32[]{:S(2)}) copy-start(f32[1088]{0:T(1024)S(1)} %convert_element_type.166) | copy-start | bytes 13060
  32.2 39.3 %copy-start.26 = (f32[256]{0:T(256)}, f32[256]{0:T(256)S(1)}, u32[]{:S(2)}) copy-start(f32[256]{0:T(256)S(1)} %broadcast_multiply_fusion.5) | copy-start | bytes 3076
  32.4 39.1 %copy-start.30 = (f32[256]{0:T(256)}, f32[256]{0:T(256)S(1)}, u32[]{:S(2)}) copy-start(f32[256]{0:T(256)S(1)} %add_rsqrt_fusion.1) | copy-start | bytes 3076
  74.1 49.7 %all-gather.19.cloned.1.call-start = ((), (), s32[]{:S(2)}) async-start(), calls=%async_computation.17 | async-start | bytes 2785280 | tf_op jit(solution)/shard_map/all_gather | solution.py:146
  76.9 87.8 %all-gather.11.cloned.1.call-start = ((), (), s32[]{:S(2)}) async-start(), calls=%async_computation.7 | async-start | bytes 3133440 | tf_op jit(solution)/shard_map/all_gather | solution.py:103
  77.5 138.5 %all-gather.13.cloned.1.call-start = ((), (), s32[]{:S(2)}) async-start(), calls=%async_computation.8 | async-start | bytes 11837440 | tf_op jit(solution)/shard_map/all_gather | solution.py:107
  78.1 206.9 %all-gather.15.cloned.1.call-start = ((), (), s32[]{:S(2)}) async-start(), calls=%async_computation.9 | async-start | bytes 12533760 | tf_op jit(solution)/shard_map/all_gather | solution.py:109
  78.7 302.7 %reduce-scatter.9.cloned.1.call-start = ((), (), s32[]{:S(2)}) async-start(), calls=%async_computation.11 | async-start | bytes 2785280 | tf_op jit(solution)/shard_map/reduce_scatter | solution.py:288
  131.8 6.6 copy-start
  167.9 128.0 %copy-start.3 = (f32[256,1088]{0,1:T(8,128)}, f32[256,1088]{0,1:T(8,128)S(1)}, u32[]{:S(2)}) copy-start(f32[256,1088]{0,1:T(8,128)S(1)} %get-tuple-element.544) | copy-start | bytes 3342340
  168.2 116.9 %copy-start.13 = (bf16[1,256,1088]{1,2,0:T(8,128)(2,1)S(1)}, bf16[1,256,1088]{1,2,0:T(8,128)(2,1)}, u32[]{:S(2)}) copy-start(bf16[1,256,1088]{1,2,0:T(8,128)(2,1)} %param.33) | copy-start | bytes 1671172
  285.0 7.9 copy-start.5
  305.6 6.2 copy-start.1
  311.9 9.1 slice-start
  335.0 9.1 slice-start
  348.9 67.4 %reduce-scatter.7.cloned.1.call-start = ((), (), s32[]{:S(2)}) async-start(), calls=%async_computation.10 | async-start | bytes 2785280 | tf_op jit(solution)/shard_map/reduce_scatter | solution.py:285
  349.7 110.9 %reduce-scatter.13.cloned.1.call-start = ((), (), s32[]{:S(2)}) async-start(), calls=%async_computation.13 | async-start | bytes 3133440 | tf_op jit(solution)/shard_map/reduce_scatter | solution.py:339
  352.7 63.7 %copy-start.15 = (bf16[1,256,1088]{1,2,0:T(8,128)(2,1)S(1)}, bf16[1,256,1088]{1,2,0:T(8,128)(2,1)}, u32[]{:S(2)}) copy-start(bf16[1,256,1088]{1,2,0:T(8,128)(2,1)} %param.19) | copy-start | bytes 1671172
  352.7 63.7 %copy-start.25 = (f32[1088]{0:T(1024)S(1)}, f32[1088]{0:T(1024)}, u32[]{:S(2)}) copy-start(f32[1088]{0:T(1024)} %copy-done.24) | copy-start | bytes 13060
  352.7 63.7 %copy-start.27 = (f32[256]{0:T(256)S(1)}, f32[256]{0:T(256)}, u32[]{:S(2)}) copy-start(f32[256]{0:T(256)} %copy-done.26) | copy-start | bytes 3076
  352.7 63.7 %copy-start.29 = (f32[1088]{0:T(1024)S(1)}, f32[1088]{0:T(1024)}, u32[]{:S(2)}) copy-start(f32[1088]{0:T(1024)} %copy-done.28) | copy-start | bytes 13060
  352.7 63.7 %copy-start.31 = (f32[256]{0:T(256)S(1)}, f32[256]{0:T(256)}, u32[]{:S(2)}) copy-start(f32[256]{0:T(256)} %copy-done.30) | copy-start | bytes 3076
  352.7 168.3 %reduce-scatter.11.cloned.1.call-start = ((), (), s32[]{:S(2)}) async-start(), calls=%async_computation.12 | async-start | bytes 9052160 | tf_op jit(solution)/shard_map/reduce_scatter | solution.py:330
  353.2 69.0 %copy-start.21 = (bf16[1,256,17,64]{1,3,2,0:T(8,128)(2,1)}, bf16[1,256,17,64]{1,3,2,0:T(8,128)(2,1)S(1)}, u32[]{:S(2)}) copy-start(bf16[1,256,17,64]{1,3,2,0:T(8,128)(2,1)S(1)} %get-tuple-element.520) | copy-start | bytes 1671172
  422.3 180.0 %reduce-scatter.15.cloned.1.call-start = ((), (), s32[]{:S(2)}) async-start(), calls=%async_computation.14 | async-start | bytes 11837440 | tf_op jit(solution)/shard_map/reduce_scatter | solution.py:351
  429.7 257.3 %reduce-scatter.17.cloned.1.call-start = ((), (), s32[]{:S(2)}) async-start(), calls=%async_computation.15 | async-start | bytes 12533760 | tf_op jit(solution)/shard_map/reduce_scatter | solution.py:357
  438.0 609.0 %all-reduce.27.cloned.1.call-start = ((), (), s32[]{:S(2)}) async-start(), calls=%async_computation.19 | async-start | bytes 14221312
  811.0 491.8 %all-reduce.25.cloned.1.call-start = ((), (), s32[]{:S(2)}) async-start(), calls=%async_computation.18 | async-start | bytes 14221312
  (29 other events, 73.6 us)
Sparse Core Ops, SparseCore 0:
  9.6 55.1 all-gather.8
  74.2 23.7 all-gather.16
  100.1 23.5 all-gather.18
  125.2 24.8 all-gather.10
  151.5 64.4 all-gather.12
  217.4 67.5 all-gather.14
  349.1 32.2 reduce-scatter.8
  384.1 32.2 reduce-scatter.6
  419.5 33.9 reduce-scatter.12
  456.1 64.8 reduce-scatter.10
  523.6 78.5 reduce-scatter.14
  604.7 82.3 reduce-scatter.16
  811.2 235.7 all-reduce.26
  1067.8 235.0 all-reduce.24
where the time goes:
time: 1360 us; the launch traced here: 1340 us
  waiting for transfers between devices  923 us (68%)
  local copies, waits for them, and re-layouts  225 us (17%)
  matrix products  122 us (9%)
  blocking collectives  25.1 us (2%)
  other arithmetic  24.7 us (2%)
  between operations  18.5 us (1%)
    unnamed x16, waiting for transfers between devices  460 us
    concatenate x1, local copies, waits for them, and re-layouts, shards(): flattened = jnp.concatenate([member.reshape(-1) for member in owned])  118 us
    reduce_scatter x1, waiting for transfers between devices, shards(): lax.psum_scatter(local_grads[11].astype(jnp.bfloat16), 'fsdp', scatter_di...  79.2 us
    reduce_scatter x1, waiting for transfers between devices, shards(): lax.psum_scatter(local_grads[9].astype(jnp.bfloat16), 'fsdp', scatter_dim...  76.8 us
    all_gather x1, waiting for transfers between devices, shards(): lax.all_gather(owned_shards[11], 'fsdp', axis=0, tiled=True)  60.8 us
    reduce_scatter x1, waiting for transfers between devices, shards(): lax.psum_scatter(local_grads[2].astype(jnp.bfloat16), 'fsdp', scatter_dim...  57.7 us
    all_gather x1, waiting for transfers between devices, shards(): lax.all_gather(owned_shards[9], 'fsdp', axis=0, tiled=True)  47.8 us
    unnamed x81, local copies, waits for them, and re-layouts  37.6 us
  transfers between devices with their start and end apart: 14, of which 12 were waited for; matrix products, arithmetic and copies ran while one was open for 9% of the time, Pallas kernels for 0%

commit v1 on v0

--- a/solution.py
+++ b/solution.py
@@ -1,3 +1,4 @@
+import functools
 import math
 
 import jax
@@ -11,6 +12,9 @@
 
 EPSILON = 1e-05
 MASKED = -1e30
+SWAP = ((0, 1), (1, 0))
+NEAR = ((0, 1), (1, 0), (2, 3), (3, 2))
+FAR = ((0, 2), (2, 0), (1, 3), (3, 1))
 
 
 def norm_rows(values, gain, shift):
@@ -62,7 +66,121 @@
     return (probs_full.astype(jnp.bfloat16), score_grads)
 
 
+class AxisComm:
+    group = "fsdp"
+    sets = "replica"
+
+    def gather(self, shard):
+        return lax.all_gather(shard, "fsdp", axis=0, tiled=True)
+
+    def reduce(self, local):
+        owned = lax.psum_scatter(local, "fsdp", scatter_dimension=0, tiled=True)
+        return lax.psum(owned, "replica").astype(jnp.float32)
+
+    def reduce_small(self, packed):
+        total = lax.psum(packed, ("replica", "fsdp"))
+        return lax.dynamic_index_in_dim(total, lax.axis_index("fsdp"), 0, keepdims=False)
+
+    def scatter_tokens(self, local):
+        return lax.psum_scatter(local, "fsdp", scatter_dimension=1, tiled=True)
+
+
+def split_half(rows):
+    size = -(-rows // 16) * 8
+    return (size, rows - size)
+
+
+def halve(array, name, pairs, place):
+    size, second = split_half(array.shape[0])
+    keep = lax.dynamic_slice_in_dim(array, place * second, size, 0)
+    send = lax.dynamic_slice_in_dim(array, (1 - place) * second, size, 0)
+    got = lax.ppermute(send, name, pairs)
+    return (keep.astype(jnp.float32) + got.astype(jnp.float32)).astype(array.dtype)
+
+
+def join(array, name, pairs, place, rows):
+    _, second = split_half(rows)
+    got = lax.ppermute(array, name, pairs)
+    low = jnp.where(place == 0, array, got)
+    high = jnp.where(place == 0, got, array)
+    return jnp.concatenate([low[:second], high], axis=0)
+
+
+class TorusComm:
+    group = ("x", "core")
+    sets = ("z", "y")
+
+    def gather(self, shard):
+        x, y, core = (lax.axis_index(name) for name in ("x", "y", "core"))
+        rows = shard.shape[0]
+        beside = lax.ppermute(shard, "core", SWAP)
+        if rows % 16 == 0:
+            half = rows // 2
+            piece = lax.dynamic_slice_in_dim(shard, y * half, half, 0)
+            got = lax.ppermute(piece, "x", SWAP)
+            other = lax.ppermute(got, "y", SWAP)
+            far = jnp.concatenate(
+                [jnp.where(y == 0, got, other), jnp.where(y == 0, other, got)], axis=0
+            )
+        else:
+            far = lax.ppermute(shard, "x", SWAP)
+        far_beside = lax.ppermute(far, "core", SWAP)
+        near_first = jnp.where(core == 0, shard, beside)
+        near_second = jnp.where(core == 0, beside, shard)
+        far_first = jnp.where(core == 0, far, far_beside)
+        far_second = jnp.where(core == 0, far_beside, far)
+        return jnp.concatenate(
+            [
+                jnp.where(x == 0, near_first, far_first),
+                jnp.where(x == 0, near_second, far_second),
+                jnp.where(x == 0, far_first, near_first),
+                jnp.where(x == 0, far_second, near_second),
+            ],
+            axis=0,
+        )
+
+    def scatter_group(self, blocks):
+        x, core = lax.axis_index("x"), lax.axis_index("core")
+        for name, place, dim in (("core", core, 1), ("x", x, 0)):
+            keep = lax.dynamic_index_in_dim(blocks, place, dim, keepdims=False)
+            send = lax.dynamic_index_in_dim(blocks, 1 - place, dim, keepdims=False)
+            got = lax.ppermute(send, name, SWAP)
+            blocks = (keep.astype(jnp.float32) + got.astype(jnp.float32)).astype(blocks.dtype)
+        return blocks
+
+    def reduce(self, local):
+        y, z = lax.axis_index("y"), lax.axis_index("z")
+        rows = local.shape[0] // 4
+        own = self.scatter_group(local.reshape(2, 2, rows, local.shape[1]))
+        steps = (("y", SWAP, y), ("z", NEAR, lax.rem(z, 2)), ("z", FAR, lax.div(z, 2)))
+        sizes = []
+        for name, pairs, place in steps:
+            sizes.append(own.shape[0])
+            own = halve(own, name, pairs, place)
+        for (name, pairs, place), size in zip(steps[::-1], sizes[::-1]):
+            own = join(own, name, pairs, place, size)
+        return own.astype(jnp.float32)
+
+    def reduce_small(self, packed):
+        for name, pairs in (
+            ("core", SWAP),
+            ("x", SWAP),
+            ("y", SWAP),
+            ("z", NEAR),
+            ("z", FAR),
+        ):
+            packed = packed + lax.ppermute(packed, name, pairs)
+        place = lax.axis_index("x") * 2 + lax.axis_index("core")
+        return lax.dynamic_index_in_dim(packed, place, 0, keepdims=False)
+
+    def scatter_tokens(self, local):
+        sequences, length, width = local.shape
+        blocks = local.reshape(sequences, 2, 2, length // 4, width)
+        return jax.vmap(self.scatter_group)(blocks)
+
+
 def shards(
+    comm,
     tokens_in,
     norm1_gain,
     norm1_bias,
@@ -79,54 +197,41 @@
     down_bias,
     out_grad,
 ):
-    owned_shards = (
+    vectors = (
         norm1_gain,
         norm1_bias,
-        qkv_weight,
         query_bias,
         value_bias,
-        out_weight,
         out_bias,
         norm2_gain,
         norm2_bias,
-        up_weight,
+        down_bias,
         up_bias,
-        down_weight,
-        down_bias,
-    )
-    gathered = (
-        lax.all_gather(owned_shards[0], "fsdp", axis=0, tiled=True),
-        lax.all_gather(owned_shards[1], "fsdp", axis=0, tiled=True),
-        lax.all_gather(owned_shards[2], "fsdp", axis=0, tiled=True),
-        lax.all_gather(owned_shards[3], "fsdp", axis=0, tiled=True),
-        lax.all_gather(owned_shards[4], "fsdp", axis=0, tiled=True),
-        lax.all_gather(owned_shards[5], "fsdp", axis=0, tiled=True),
-        lax.all_gather(owned_shards[6], "fsdp", axis=0, tiled=True),
-        lax.all_gather(owned_shards[7], "fsdp", axis=0, tiled=True),
-        lax.all_gather(owned_shards[8], "fsdp", axis=0, tiled=True),
-        lax.all_gather(owned_shards[9], "fsdp", axis=0, tiled=True),
-        lax.all_gather(owned_shards[10], "fsdp", axis=0, tiled=True),
-        lax.all_gather(owned_shards[11], "fsdp", axis=0, tiled=True),
-        lax.all_gather(owned_shards[12], "fsdp", axis=0, tiled=True),
-    )
+    )
+    members = lax.axis_size(comm.group)
+    every = lax.all_gather(jnp.concatenate(vectors), comm.group, axis=0)
+    pieces, position = [], 0
+    for member in vectors:
+        pieces.append(every[:, position : position + member.size].reshape(-1))
+        position = position + member.size
     (
         first_gain,
         first_shift,
-        full_qkv,
         query_shift,
         value_shift,
-        full_out,
         out_shift,
         second_gain,
         second_shift,
-        full_up,
+        down_shift,
         up_shift,
-        full_down,
-        down_shift,
-    ) = gathered
+    ) = pieces
+    full_qkv = comm.gather(qkv_weight)
+    full_out = comm.gather(out_weight)
+    full_up = comm.gather(up_weight)
+    full_down = comm.gather(down_weight)
     sequences, local_len, model_width = tokens_in.shape
     row_count = sequences * local_len
-    device_index = lax.axis_index("fsdp")
+    device_index = lax.axis_index(comm.group)
     factor = 1.0 / math.sqrt(HEAD_DIM)
     inputs = tokens_in.astype(jnp.float32).reshape(row_count, model_width)
     scaled_one, inverse_one, normed_one = norm_rows(
@@ -139,14 +244,13 @@
     value_rows = (projected[:, 2 * model_width :] + value_shift.astype(jnp.float32)).astype(
         jnp.bfloat16
     )
-    key_all, value_all = (
-        lax.all_gather(
-            key_rows.reshape(sequences, local_len, model_width), "fsdp", axis=1, tiled=True
-        ),
-        lax.all_gather(
-            value_rows.reshape(sequences, local_len, model_width), "fsdp", axis=1, tiled=True
-        ),
-    )
+    both_all = lax.all_gather(
+        jnp.stack([key_rows, value_rows]).reshape(2, sequences, local_len, model_width),
+        comm.group,
+        axis=2,
+        tiled=True,
+    )
+    key_all, value_all = both_all[0], both_all[1]
     full_len = key_all.shape[1]
     key_block = min(512, full_len)
     key_turns = full_len // key_block
@@ -213,11 +317,19 @@
     back_gain_two, back_up, back_down = (second_gain, full_up, full_down)
     upstream = out_grad.reshape(row_count, model_width)
     upstream_full = upstream.astype(jnp.float32)
-    grad_down = jnp.einsum("rf,rd->fd", hidden, upstream, preferred_element_type=jnp.float32)
+    grad_down = comm.reduce(
+        jnp.einsum("rf,rd->fd", hidden, upstream, preferred_element_type=jnp.float32).astype(
+            jnp.bfloat16
+        )
+    )
     grad_down_shift = jnp.sum(upstream_full, axis=0)
     hidden_grad = jnp.einsum("rd,fd->rf", upstream, back_down, preferred_element_type=jnp.float32)
     pre_grad = gelu_pull(hidden_grad)[0].astype(jnp.bfloat16)
-    grad_up = jnp.einsum("rd,rf->df", second_low, pre_grad, preferred_element_type=jnp.float32)
+    grad_up = comm.reduce(
+        jnp.einsum("rd,rf->df", second_low, pre_grad, preferred_element_type=jnp.float32).astype(
+            jnp.bfloat16
+        )
+    )
     grad_up_shift = jnp.sum(pre_grad.astype(jnp.float32), axis=0)
     second_grad = jnp.einsum("rf,df->rd", pre_grad, back_up, preferred_element_type=jnp.float32)
     middle_norm_grad, grad_second_gain, grad_second_shift = norm_back(
@@ -225,7 +337,11 @@
     )
     middle_grad = upstream_full + middle_norm_grad
     middle_low = middle_grad.astype(jnp.bfloat16)
-    grad_out = jnp.einsum("re,rd->ed", attended_low, middle_low, preferred_element_type=jnp.float32)
+    grad_out = comm.reduce(
+        jnp.einsum("re,rd->ed", attended_low, middle_low, preferred_element_type=jnp.float32).astype(
+            jnp.bfloat16
+        )
+    )
     grad_out_shift = jnp.sum(middle_low.astype(jnp.float32), axis=0)
     attended_grad = jnp.einsum(
         "rd,ed->re", middle_low, back_out, preferred_element_type=jnp.float32
@@ -281,23 +397,23 @@
         jnp.zeros((sequences, full_len, model_width), jnp.float32),
     )
     query_grad, key_grads, value_grads = lax.fori_loop(0, key_turns, backward_step, start_back)
-    own_key_grad, own_value_grad = (
-        lax.psum_scatter(
-            key_grads.astype(jnp.bfloat16), "fsdp", scatter_dimension=1, tiled=True
-        ).astype(jnp.float32),
-        lax.psum_scatter(
-            value_grads.astype(jnp.bfloat16), "fsdp", scatter_dimension=1, tiled=True
-        ).astype(jnp.float32),
-    )
-    qkv_grad = jnp.concatenate(
+    query_low = query_grad.reshape(row_count, model_width).astype(jnp.bfloat16)
+    own_both = comm.scatter_tokens(
+        jnp.concatenate([key_grads, value_grads], axis=0).astype(jnp.bfloat16)
+    ).reshape(2, row_count, model_width)
+    qkv_grad = jnp.concatenate([query_low, own_both[0], own_both[1]], axis=1)
+    early = model_width // 128 * 128
+    grad_qkv = jnp.concatenate(
         [
-            query_grad.reshape(row_count, model_width),
-            own_key_grad.reshape(row_count, model_width),
-            own_value_grad.reshape(row_count, model_width),
+            comm.reduce(
+                jnp.einsum(
+                    "rd,rc->dc", normed_low, part, preferred_element_type=jnp.float32
+                ).astype(jnp.bfloat16)
+            )
+            for part in (query_low[:, :early], qkv_grad[:, early:])
         ],
         axis=1,
-    ).astype(jnp.bfloat16)
-    grad_qkv = jnp.einsum("rd,rc->dc", normed_low, qkv_grad, preferred_element_type=jnp.float32)
+    )
     grad_query_shift = jnp.sum(qkv_grad[:, :model_width].astype(jnp.float32), axis=0)
     grad_value_shift = jnp.sum(qkv_grad[:, 2 * model_width :].astype(jnp.float32), axis=0)
     first_grad = jnp.einsum("rc,dc->rd", qkv_grad, back_qkv, preferred_element_type=jnp.float32)
@@ -305,132 +421,86 @@
         first_grad, scaled_one, inverse_one, back_gain_one.astype(jnp.float32)
     )
     input_grad = (middle_grad + input_norm_grad).reshape(sequences, local_len, model_width)
-    local_grads = (
+    small = (
         grad_first_gain,
         grad_first_shift,
-        grad_qkv,
         grad_query_shift,
         grad_value_shift,
-        grad_out,
         grad_out_shift,
         grad_second_gain,
         grad_second_shift,
-        grad_up,
+        grad_down_shift,
         grad_up_shift,
-        grad_down,
-        grad_down_shift,
-    )
-    owned = (
-        lax.psum_scatter(
-            local_grads[0].astype(jnp.bfloat16), "fsdp", scatter_dimension=0, tiled=True
-        ).astype(jnp.float32),
-        lax.psum_scatter(
-            local_grads[1].astype(jnp.bfloat16), "fsdp", scatter_dimension=0, tiled=True
-        ).astype(jnp.float32),
-        lax.psum_scatter(
-            local_grads[2].astype(jnp.bfloat16), "fsdp", scatter_dimension=0, tiled=True
-        ).astype(jnp.float32),
-        lax.psum_scatter(
-            local_grads[3].astype(jnp.bfloat16), "fsdp", scatter_dimension=0, tiled=True
-        ).astype(jnp.float32),
-        lax.psum_scatter(
-            local_grads[4].astype(jnp.bfloat16), "fsdp", scatter_dimension=0, tiled=True
-        ).astype(jnp.float32),
-        lax.psum_scatter(
-            local_grads[5].astype(jnp.bfloat16), "fsdp", scatter_dimension=0, tiled=True
-        ).astype(jnp.float32),
-        lax.psum_scatter(
-            local_grads[6].astype(jnp.bfloat16), "fsdp", scatter_dimension=0, tiled=True
-        ).astype(jnp.float32),
-        lax.psum_scatter(
-            local_grads[7].astype(jnp.bfloat16), "fsdp", scatter_dimension=0, tiled=True
-        ).astype(jnp.float32),
-        lax.psum_scatter(
-            local_grads[8].astype(jnp.bfloat16), "fsdp", scatter_dimension=0, tiled=True
-        ).astype(jnp.float32),
-        lax.psum_scatter(
-            local_grads[9].astype(jnp.bfloat16), "fsdp", scatter_dimension=0, tiled=True
-        ).astype(jnp.float32),
-        lax.psum_scatter(
-            local_grads[10].astype(jnp.bfloat16), "fsdp", scatter_dimension=0, tiled=True
-        ).astype(jnp.float32),
-        lax.psum_scatter(
-            local_grads[11].astype(jnp.bfloat16), "fsdp", scatter_dimension=0, tiled=True
-        ).astype(jnp.float32),
-        lax.psum_scatter(
-            local_grads[12].astype(jnp.bfloat16), "fsdp", scatter_dimension=0, tiled=True
-        ).astype(jnp.float32),
-    )
-    flattened = jnp.concatenate([member.reshape(-1) for member in owned])
-    share = lax.psum_scatter(
-        flattened.astype(jnp.bfloat16), "replica", scatter_dimension=0, tiled=True
-    ).astype(jnp.float32)
-    summed_all = lax.all_gather(share.astype(jnp.bfloat16), "replica", axis=0, tiled=True).astype(
-        share.dtype
-    )
-    totals = []
-    position = 0
-    for member in owned:
-        length_of = member.size
-        totals.append(summed_all[position : position + length_of].reshape(member.shape))
-        position = position + length_of
+    )
+    packed = jnp.concatenate([member.reshape(members, -1) for member in small], axis=1)
+    summed_small = comm.reduce_small(packed)
+    totals, position = [], 0
+    for member in small:
+        totals.append(summed_small[position : position + member.size // members])
+        position = position + member.size // members
     return (
         block_out,
         input_grad,
         totals[0],
         totals[1],
+        grad_qkv,
         totals[2],
         totals[3],
+        grad_out,
         totals[4],
         totals[5],
         totals[6],
+        grad_up,
+        totals[8],
+        grad_down,
         totals[7],
-        totals[8],
-        totals[9],
-        totals[10],
-        totals[11],
-        totals[12],
     )
 
 
 def solution(mesh):
+    comm, whole = AxisComm(), mesh
+    if dict(mesh.shape) == {"replica": 8, "fsdp": 4}:
+        comm = TorusComm()
+        whole = jax.sharding.Mesh(mesh.devices.reshape(4, 2, 2, 2), ("z", "y", "x", "core"))
+    sets, group = comm.sets, comm.group
+    tokens, rows, vector = P(sets, group, None), P(group, None), P(group)
     placed = (
-        P("replica", "fsdp", None),
-        P("fsdp"),
-        P("fsdp"),
-        P("fsdp", None),
-        P("fsdp"),
-        P("fsdp"),
-        P("fsdp", None),
-        P("fsdp"),
-        P("fsdp"),
-        P("fsdp"),
-        P("fsdp", None),
-        P("fsdp"),
-        P("fsdp", None),
-        P("fsdp"),
-        P("replica", "fsdp", None),
+        tokens,
+        vector,
+        vector,
+        rows,
+        vector,
+        vector,
+        rows,
+        vector,
+        vector,
+        vector,
+        rows,
+        vector,
+        rows,
+        vector,
+        tokens,
     )
     return jax.shard_map(
-        shards,
-        mesh=mesh,
+        functools.partial(shards, comm),
+        mesh=whole,
         in_specs=placed,
         out_specs=(
-            P("replica", "fsdp", None),
-            P("replica", "fsdp", None),
-            P("fsdp"),
-            P("fsdp"),
-            P("fsdp", None),
-            P("fsdp"),
-            P("fsdp"),
-            P("fsdp", None),
-            P("fsdp"),
-            P("fsdp"),
-            P("fsdp"),
-            P("fsdp", None),
-            P("fsdp"),
-            P("fsdp", None),
-            P("fsdp"),
+            tokens,
+            tokens,
+            vector,
+            vector,
+            rows,
+            vector,
+            vector,
+            rows,
+            vector,
+            vector,
+            vector,
+            rows,
+            vector,
+            rows,
+            vector,
         ),
         check_vma=False,
     )

time: 1360 us -> 874 us (0.64)
  waiting for transfers between devices: 923 us -> 353 us
  other arithmetic: 24.7 us -> 98.4 us
  local copies, waits for them, and re-layouts: 225 us -> 168 us
  starting transfers between devices: 1.12 us -> 52.2 us
  blocking collectives: 25.1 us -> 53.8 us
    unnamed x16 -> x1, waiting for transfers between devices: 460 us -> 0.02 us
    ppermute x0 -> x63, waiting for transfers between devices: none -> 353 us  [the longest x12 102 us: scatter_group(): got = lax.ppermute(send, name, SWAP)]
    reduce_scatter x6 -> x0, waiting for transfers between devices: 277 us -> none  [the longest x1 79.2 us: shards(): lax.psum_scatter(local_grads[11].astype(jnp.bfloat16), 'fsdp', scatter_di...]
    all_gather x6 -> x1, waiting for transfers between devices: 186 us -> 0.01 us  [shards(): lax.all_gather(jnp.stack([key_rows, value_rows]).reshape(2, sequences, lo...]
    concatenate x1 -> x6, local copies, waits for them, and re-layouts: 118 us -> 9.01 us  [the longest x2 7.61 us: shards(): jnp.concatenate([key_grads, value_grads], axis=0).astype(jnp.bfloat16)]
    dynamic_slice x0 -> x21, local copies, waits for them, and re-layouts: none -> 52.4 us  [the longest x1 23.4 us: scatter_group(): send = lax.dynamic_index_in_dim(blocks, 1 - place, dim, keepdims=False)]
    ppermute x0 -> x63, starting transfers between devices: none -> 52.2 us  [the longest x15 20.4 us: halve(): got = lax.ppermute(send, name, pairs)]
    select_n x0 -> x31, other arithmetic: none -> 38.3 us  [the longest x4 26.8 us: gather(): jnp.where(x == 0, near_first, far_first)]
  transfers between devices with their start and end apart: 14 -> 64, of which waited for: 12 -> 31; matrix products, arithmetic and copies ran while one was open for 9% -> 24% of each run, Pallas kernels for 0% -> 0%
where the time goes in v1:
time: 874 us; the launch traced here: 861 us
  waiting for transfers between devices  353 us (40%)
  local copies, waits for them, and re-layouts  168 us (19%)
  matrix products  119 us (14%)
  other arithmetic  98.4 us (11%)
  blocking collectives  53.8 us (6%)
  starting transfers between devices  52.2 us (6%)
  between operations  16.7 us (2%)
    ppermute x12, waiting for transfers between devices, scatter_group(): got = lax.ppermute(send, name, SWAP)  102 us
    ppermute x15, waiting for transfers between devices, join(): got = lax.ppermute(array, name, pairs)  94.4 us
    ppermute x15, waiting for transfers between devices, halve(): got = lax.ppermute(send, name, pairs)  85.7 us
    ppermute x4, waiting for transfers between devices, gather(): other = lax.ppermute(got, 'y', SWAP)  57.2 us
    unnamed x1, blocking collectives  53.8 us
    unnamed x188, local copies, waits for them, and re-layouts  34.4 us
    select_n x4, other arithmetic, gather(): jnp.where(x == 0, near_first, far_first)  26.8 us
    convert_element_type x12, other arithmetic, scatter_group(): (keep.astype(jnp.float32) + got.astype(jnp.float32)).astype(blocks.dtype)  23.7 us
  transfers between devices with their start and end apart: 64, of which 31 were waited for; matrix products, arithmetic and copies ran while one was open for 24% of the time, Pallas kernels for 0%

profile of v1, /device:TPU:0, one launch (start us, length us, event | category | flops | bytes accessed | tf_op | source)
XLA Modules:
  0.0 861.3 jit_solution(12165837578083673310)
XLA Ops:
  19.1 53.8 %all-reduce.2 = bf16[13056]{0:T(1024)(128)(2,1)S(1)} all-reduce(bf16[13056]{0:T(1024)(128)(2,1)S(1)} %dynamic-update-slice.4), channel_id=2, replica_groups=mesh['z'=4,'y'=2,'x'=2,'core'=2] {'x','core'}, use_global_device_ids=true, to_apply=%add.2 | all-reduce | flops 13056 | bytes 52224
  83.9 10.6 %collective-permute-done.2 = bf16[136,3264]{1,0:T(8,128)(2,1)} collective-permute-done((bf16[136,3264]{1,0:T(8,128)(2,1)}, bf16[136,3264]{1,0:T(8,128)(2,1)}, u32[]{:S(2)}, u32[]{:S(2)}) %collective-permute-start.2) | collective-permute-done | bytes 887840 | tf_op jit(solution)/shard_map/ppermute | solution.py:121
  97.9 22.5 %collective-permute-done.10 = bf16[136,4352]{1,0:T(8,128)(2,1)S(1)} collective-permute-done((bf16[136,4352]{1,0:T(8,128)(2,1)S(1)}, bf16[136,4352]{1,0:T(8,128)(2,1)S(1)}, u32[]{:S(2)}, u32[]{:S(2)}) %collective-permute-start.10) | collective-permute-done | bytes 1183776 | tf_op jit(solution)/shard_map/ppermute | solution.py:121
  136.8 24.1 %collective-permute-done.14 = bf16[544,1088]{1,0:T(8,128)(2,1)} collective-permute-done((bf16[544,1088]{1,0:T(8,128)(2,1)}, bf16[544,1088]{1,0:T(8,128)(2,1)}, u32[]{:S(2)}, u32[]{:S(2)}) %collective-permute-start.14) | collective-permute-done | bytes 1183776 | tf_op jit(solution)/shard_map/ppermute | solution.py:121
  168.0 8.1 broadcast_select_fusion.15
  176.1 12.1 %broadcast_select_fusion.7 = (bf16[1088,1088]{1,0:T(8,128)(2,1)}, bf16[1088,1088]{1,0:T(8,128)(2,1)}, bf16[1088,1088]{1,0:T(8,128)(2,1)}, bf16[1088,1088]{1,0:T(8,128)(2,1)}) fusion(pred[]{:T(512)S(6)} %eq.10, bf16[1088,1088]{1,0:T(8,128)(2,1)} %param.31, bf16[1088,1088]{1,0:T(8,128)(2,1)} %collective-permute-done.12, pred[]{:T(512)S(6)} %eq.11, ...), kind=kLoop, calls=%fused_computation.111 | loop fusion | flops 14204928 | bytes 18939906 | tf_op jit(solution)/shard_map/jit(_where)/select_n | solution.py:134
  192.3 37.5 %while.40 = (s32[]{:T(128)}, f32[1,17,256]{2,1,0:T(8,128)S(1)}, f32[1,17,256]{2,1,0:T(8,128)S(1)}, f32[1,17,256,64]{2,3,1,0:T(8,128)}, bf16[1,1024,1088]{1,2,0:T...) while((s32[]{:T(128)}, f32[1,17,256]{2,1,0:T(8,128)S(1)}, ...), condition=%wide.region_5.6_spmd.clone, body=%wide.region_2.5_spmd.clone.sunk | while | flops 595929344 | bytes 72669408 | solution.py:292
  236.1 6.8 multiply_convert_fusion
  242.9 15.6 %convert_reduce_fusion = (f32[4352]{0:T(1024)}, bf16[256,4352]{1,0:T(8,128)(2,1)}) fusion(f32[256,4352]{1,0:T(8,128)} %get-tuple-element.621, bf16[1,256,1088]{1,2,0:T(8,128)(2,1)S(1)} %copy-done.29, bf16[1088,1088]{1,0:T(8,128)(2,1)} %get-tuple-element.566, bf16[1088,1088]{1,0:T(8,128)(2,1)} %get-tuple-element.565, ...), kind=kOutput, calls=%fused_computation.83 | convolution fusion | flops 2478894848 | bytes 16729088 | tf_op jit(solution)/shard_map/rd,fd->rf/dot_general | solution.py:326
  258.5 7.3 multiply_reduce_fusion
  279.9 52.9 %while.41 = (s32[]{:T(128)}, f32[1,256,17,64]{1,3,2,0:T(8,128)}, bf16[1,1024,1088]{1,2,0:T(8,128)(2,1)}, bf16[1,1024,1088]{1,2,0:T(8,128)(2,1)}, bf16[1,1024,108...) while((s32[]{:T(128)}, f32[1,256,17,64]{1,3,2,0:T(8,128)}, ...), condition=%wide.region_12.13_spmd.clone, body=%wide.region_11.12_spmd.clone.sunk | while | flops 1450427136 | bytes 175507088 | solution.py:399
  295.6 6.1 fusion.182
  356.5 6.6 fusion.55
  379.3 16.8 %reshape.500 = bf16[2,2,1088,1088]{2,1,0,3:T(2,128)(2,1)} reshape(bf16[4352,1088]{0,1:T(8,128)(2,1)} %convolution_convert_fusion) | data formatting | bytes 18939904 | tf_op jit(solution)/shard_map/reshape | solution.py:154
  428.8 7.4 collective-permute-done.43
  450.2 22.5 %constant_dynamic-slice_fusion.9 = (bf16[2,1,1088,1088]{2,1,0,3:T(2,128)(2,1)}, bf16[2,1,1088,1088]{2,1,0,3:T(2,128)(2,1)}) fusion(bf16[2,2,1088,1088]{2,1,0,3:T(2,128)(2,1)S(1)} %bitcast.341, s32[]{:T(128)} %select_n.559, s32[]{:T(128)} %select_n.560), kind=kLoop, calls=%fused_computation.302 | loop fusion | bytes 18939912 | tf_op jit(solution)/shard_map/jit(dynamic_index_in_dim)/dynamic_slice | solution.py:145
  472.7 23.4 %copy.82 = bf16[2,1,1088,1088]{3,2,0,1:T(8,128)(2,1)} copy(bf16[2,1,1088,1088]{2,1,0,3:T(2,128)(2,1)} %get-tuple-element.562) | data formatting | bytes 9469952 | tf_op jit(solution)/shard_map/jit(dynamic_index_in_dim)/dynamic_slice | solution.py:146
  496.0 23.5 %copy.92 = bf16[2,1,1088,1088]{3,2,0,1:T(8,128)(2,1)} copy(bf16[2,1,1088,1088]{2,1,0,3:T(2,128)(2,1)} %get-tuple-element.561) | data formatting | bytes 9469952
  570.1 70.4 %collective-permute-done.32 = bf16[272,2240]{1,0:T(8,128)(2,1)} collective-permute-done((bf16[272,2240]{1,0:T(8,128)(2,1)}, bf16[272,2240]{1,0:T(8,128)(2,1)}, u32[]{:S(2)}, u32[]{:S(2)}) %collective-permute-start.32) | collective-permute-done | bytes 1218592 | tf_op jit(solution)/shard_map/ppermute | solution.py:147
  646.7 12.6 %collective-permute-done.33 = bf16[136,2240]{1,0:T(8,128)(2,1)S(1)} collective-permute-done((bf16[136,2240]{1,0:T(8,128)(2,1)S(1)}, bf16[136,2240]{1,0:T(8,128)(2,1)S(1)}, u32[]{:S(2)}, u32[]{:S(2)}) %collective-permute-start.33) | collective-permute-done | bytes 609312 | tf_op jit(solution)/shard_map/ppermute | solution.py:97
  659.6 28.9 %collective-permute-done.56 = bf16[1088,1088]{1,0:T(8,128)(2,1)S(1)} collective-permute-done((bf16[1088,1088]{1,0:T(8,128)(2,1)S(1)}, bf16[1088,1088]{1,0:T(8,128)(2,1)S(1)}, u32[]{:S(2)}, u32[]{:S(2)}) %collective-permute-start.56) | collective-permute-done | bytes 2367520 | tf_op jit(solution)/shard_map/ppermute | solution.py:147
  692.0 9.7 %collective-permute-done.35 = bf16[40,2240]{1,0:T(8,128)(2,1)S(1)} collective-permute-done((bf16[40,2240]{1,0:T(8,128)(2,1)S(1)}, bf16[40,2240]{1,0:T(8,128)(2,1)S(1)}, u32[]{:S(2)}, u32[]{:S(2)}) %collective-permute-start.35) | collective-permute-done | bytes 179232 | tf_op jit(solution)/shard_map/ppermute | solution.py:97
  709.3 7.6 collective-permute-done.57
  718.2 9.0 %collective-permute-done.37 = bf16[72,2240]{1,0:T(8,128)(2,1)S(1)} collective-permute-done((bf16[72,2240]{1,0:T(8,128)(2,1)S(1)}, bf16[72,2240]{1,0:T(8,128)(2,1)S(1)}, u32[]{:S(2)}, u32[]{:S(2)}) %collective-permute-start.37) | collective-permute-done | bytes 322592 | tf_op jit(solution)/shard_map/ppermute | solution.py:103
  728.0 8.8 %collective-permute-done.58 = bf16[272,1088]{1,0:T(8,128)(2,1)S(1)} collective-permute-done((bf16[272,1088]{1,0:T(8,128)(2,1)S(1)}, bf16[272,1088]{1,0:T(8,128)(2,1)S(1)}, u32[]{:S(2)}, u32[]{:S(2)}) %collective-permute-start.58) | collective-permute-done | bytes 591904 | tf_op jit(solution)/shard_map/ppermute | solution.py:97
  740.4 19.1 %collective-permute-done.59 = bf16[136,1088]{1,0:T(8,128)(2,1)S(1)} collective-permute-done((bf16[136,1088]{1,0:T(8,128)(2,1)S(1)}, bf16[136,1088]{1,0:T(8,128)(2,1)S(1)}, u32[]{:S(2)}, u32[]{:S(2)}) %collective-permute-start.59) | collective-permute-done | bytes 295968 | tf_op jit(solution)/shard_map/ppermute | solution.py:97
  762.0 12.1 %collective-permute-done.51 = bf16[40,4352]{1,0:T(8,128)(2,1)S(1)} collective-permute-done((bf16[40,4352]{1,0:T(8,128)(2,1)S(1)}, bf16[40,4352]{1,0:T(8,128)(2,1)S(1)}, u32[]{:S(2)}, u32[]{:S(2)}) %collective-permute-start.51) | collective-permute-done | bytes 348192 | tf_op jit(solution)/shard_map/ppermute | solution.py:97
  774.2 10.4 %collective-permute-done.60 = bf16[136,1088]{1,0:T(8,128)(2,1)S(1)} collective-permute-done((bf16[136,1088]{1,0:T(8,128)(2,1)S(1)}, bf16[136,1088]{1,0:T(8,128)(2,1)S(1)}, u32[]{:S(2)}, u32[]{:S(2)}) %collective-permute-start.60) | collective-permute-done | bytes 295968 | tf_op jit(solution)/shard_map/ppermute | solution.py:103
  789.3 13.3 %collective-permute-done.61 = bf16[272,1088]{1,0:T(8,128)(2,1)S(1)} collective-permute-done((bf16[272,1088]{1,0:T(8,128)(2,1)S(1)}, bf16[272,1088]{1,0:T(8,128)(2,1)S(1)}, u32[]{:S(2)}, u32[]{:S(2)}) %collective-permute-start.61) | collective-permute-done | bytes 591904 | tf_op jit(solution)/shard_map/ppermute | solution.py:103
  803.5 9.3 %collective-permute-done.53 = bf16[72,4352]{1,0:T(8,128)(2,1)S(1)} collective-permute-done((bf16[72,4352]{1,0:T(8,128)(2,1)S(1)}, bf16[72,4352]{1,0:T(8,128)(2,1)S(1)}, u32[]{:S(2)}, u32[]{:S(2)}) %collective-permute-start.53) | collective-permute-done | bytes 626720 | tf_op jit(solution)/shard_map/ppermute | solution.py:103
  813.5 19.9 %collective-permute-done.62 = bf16[544,1088]{1,0:T(8,128)(2,1)S(1)} collective-permute-done((bf16[544,1088]{1,0:T(8,128)(2,1)S(1)}, bf16[544,1088]{1,0:T(8,128)(2,1)S(1)}, u32[]{:S(2)}, u32[]{:S(2)}) %collective-permute-start.62) | collective-permute-done | bytes 1183776 | tf_op jit(solution)/shard_map/ppermute | solution.py:103
  836.6 14.7 %collective-permute-done.54 = bf16[136,4352]{1,0:T(8,128)(2,1)S(1)} collective-permute-done((bf16[136,4352]{1,0:T(8,128)(2,1)S(1)}, bf16[136,4352]{1,0:T(8,128)(2,1)S(1)}, u32[]{:S(2)}, u32[]{:S(2)}) %collective-permute-start.54) | collective-permute-done | bytes 1183776 | tf_op jit(solution)/shard_map/ppermute | solution.py:103
  (590 shorter events, 330.5 us)
Async XLA Ops:
  7.2 181.0 %all-gather.4.cloned.1.call-start = ((), (), s32[]{:S(2)}) async-start(), calls=%async_computation | async-start | bytes 5570560 | tf_op jit(solution)/shard_map/all_gather | solution.py:247
  7.2 116.8 %collective-permute-start = (bf16[272,3264]{1,0:T(8,128)(2,1)}, bf16[272,3264]{1,0:T(8,128)(2,1)}, u32[]{:S(2)}, u32[]{:S(2)}) collective-permute-start(bf16[272,3264]{1,0:T(8,128)(2,1)} %param.22), channel_id=1, source_target_pairs={{0,1},{1,0},{2,3},{3,2},{4,5},{5,4},{6,7},{7,6},{8,9},{9,8},{10,11... | collective-permute-start | bytes 5326856 | tf_op jit(solution)/shard_map/ppermute | solution.py:116
  10.1 63.3 %collective-permute-start.1 = (bf16[136,3264]{1,0:T(8,128)(2,1)}, bf16[136,3264]{1,0:T(8,128)(2,1)}, u32[]{:S(2)}, u32[]{:S(2)}) collective-permute-start(bf16[136,3264]{1,0:T(8,128)(2,1)} %constant_dynamic-slice_fusion.26), channel_id=1, source_target_pairs={{0,2},{2,0},{1,3},{3,1},{4,6},{6,4},{5,7},{7,5},{8,10},{10,8},{9,1... | collective-permute-start | bytes 2663432 | tf_op jit(solution)/shard_map/ppermute | solution.py:120
  12.6 150.5 %collective-permute-start.4 = (bf16[272,1088]{1,0:T(8,128)(2,1)}, bf16[272,1088]{1,0:T(8,128)(2,1)}, u32[]{:S(2)}, u32[]{:S(2)}) collective-permute-start(bf16[272,1088]{1,0:T(8,128)(2,1)} %param.25), channel_id=1, source_target_pairs={{0,1},{1,0},{2,3},{3,2},{4,5},{5,4},{6,7},{7,6},{8,9},{9,8},{10,11... | collective-permute-start | bytes 1775624 | tf_op jit(solution)/shard_map/ppermute | solution.py:116
  13.8 109.7 %collective-permute-start.5 = (bf16[136,1088]{1,0:T(8,128)(2,1)S(1)}, bf16[136,1088]{1,0:T(8,128)(2,1)}, u32[]{:S(2)}, u32[]{:S(2)}) collective-permute-start(bf16[136,1088]{1,0:T(8,128)(2,1)S(1)} %constant_dynamic-slice_fusion.25), channel_id=1, source_target_pairs={{0,2},{2,0},{1,3},{3,1},{4,6},{6,4},{5,7},{7,5},{8,10},{10,8},{9,1... | collective-permute-start | bytes 887816 | tf_op jit(solution)/shard_map/ppermute | solution.py:120
  15.5 67.8 %collective-permute-start.9 = (bf16[136,4352]{1,0:T(8,128)(2,1)S(1)}, bf16[136,4352]{1,0:T(8,128)(2,1)S(1)}, u32[]{:S(2)}, u32[]{:S(2)}) collective-permute-start(bf16[136,4352]{1,0:T(8,128)(2,1)S(1)} %constant_dynamic-slice_fusion.24), channel_id=1, source_target_pairs={{0,2},{2,0},{1,3},{3,1},{4,6},{6,4},{5,7},{7,5},{8,10},{10,8},{9,1... | collective-permute-start | bytes 3551240 | tf_op jit(solution)/shard_map/ppermute | solution.py:120
  83.3 40.7 %collective-permute-start.13 = (bf16[544,1088]{1,0:T(8,128)(2,1)S(1)}, bf16[544,1088]{1,0:T(8,128)(2,1)}, u32[]{:S(2)}, u32[]{:S(2)}) collective-permute-start(bf16[544,1088]{1,0:T(8,128)(2,1)S(1)} %constant_dynamic-slice_fusion.23), channel_id=1, source_target_pairs={{0,2},{2,0},{1,3},{3,1},{4,6},{6,4},{5,7},{7,5},{8,10},{10,8},{9,1... | collective-permute-start | bytes 3551240 | tf_op jit(solution)/shard_map/ppermute | solution.py:120
  94.4 26.0 %collective-permute-start.10 = (bf16[136,4352]{1,0:T(8,128)(2,1)S(1)}, bf16[136,4352]{1,0:T(8,128)(2,1)S(1)}, u32[]{:S(2)}, u32[]{:S(2)}) collective-permute-start(bf16[136,4352]{1,0:T(8,128)(2,1)S(1)} %collective-permute-done.9), channel_id=1, source_target_pairs={{0,4},{4,0},{1,5},{5,1},{2,6},{6,2},{3,7},{7,3},{8,12},{12,8},{9,1... | collective-permute-start | bytes 3551240 | tf_op jit(solution)/shard_map/ppermute | solution.py:121
  123.4 44.6 %collective-permute-start.8 = (bf16[272,4352]{1,0:T(8,128)(2,1)}, bf16[272,4352]{1,0:T(8,128)(2,1)}, u32[]{:S(2)}, u32[]{:S(2)}) collective-permute-start(bf16[272,4352]{1,0:T(8,128)(2,1)} %param.29), channel_id=1, source_target_pairs={{0,1},{1,0},{2,3},{3,2},{4,5},{5,4},{6,7},{7,6},{8,9},{9,8},{10,11... | collective-permute-start | bytes 7102472 | tf_op jit(solution)/shard_map/ppermute | solution.py:116
  124.0 52.1 %collective-permute-start.12 = (bf16[1088,1088]{1,0:T(8,128)(2,1)}, bf16[1088,1088]{1,0:T(8,128)(2,1)}, u32[]{:S(2)}, u32[]{:S(2)}) collective-permute-start(bf16[1088,1088]{1,0:T(8,128)(2,1)} %param.31), channel_id=1, source_target_pairs={{0,1},{1,0},{2,3},{3,2},{4,5},{5,4},{6,7},{7,6},{8,9},{9,8},{10,11... | collective-permute-start | bytes 7102472 | tf_op jit(solution)/shard_map/ppermute | solution.py:116
  125.8 35.2 %collective-permute-start.14 = (bf16[544,1088]{1,0:T(8,128)(2,1)}, bf16[544,1088]{1,0:T(8,128)(2,1)}, u32[]{:S(2)}, u32[]{:S(2)}) collective-permute-start(bf16[544,1088]{1,0:T(8,128)(2,1)} %collective-permute-done.13), channel_id=1, source_target_pairs={{0,4},{4,0},{1,5},{5,1},{2,6},{6,2},{3,7},{7,3},{8,12},{12,8},{9,1... | collective-permute-start | bytes 3551240 | tf_op jit(solution)/shard_map/ppermute | solution.py:121
  135.6 32.5 %collective-permute-start.11 = (bf16[272,4352]{1,0:T(8,128)(2,1)}, bf16[272,4352]{1,0:T(8,128)(2,1)S(1)}, u32[]{:S(2)}, u32[]{:S(2)}) collective-permute-start(bf16[272,4352]{1,0:T(8,128)(2,1)} %pad_maximum_fusion.5), channel_id=1, source_target_pairs={{0,1},{1,0},{2,3},{3,2},{4,5},{5,4},{6,7},{7,6},{8,9},{9,8},{10,11... | collective-permute-start | bytes 7102472 | tf_op jit(solution)/shard_map/ppermute | solution.py:127
  352.9 69.8 %collective-permute-start.16 = (bf16[2,2,256,1088]{2,3,0,1:T(8,128)(2,1)}, bf16[2,2,256,1088]{2,3,0,1:T(8,128)(2,1)}, u32[]{:S(2)}, u32[]{:S(2)}) collective-permute-start(bf16[2,2,256,1088]{2,3,0,1:T(8,128)(2,1)} %fusion.57), channel_id=1, source_target_pairs={{0,1},{1,0},{2,3},{3,2},{4,5},{5,4},{6,7},{7,6},{8,9},{9,8},{10,11... | collective-permute-start | bytes 6684680 | tf_op jit(solution)/shard_map/vmap()/ppermute | solution.py:147
  372.5 23.6 %collective-permute-start.24 = (bf16[272,1024]{1,0:T(8,128)(2,1)}, bf16[272,1024]{1,0:T(8,128)(2,1)}, u32[]{:S(2)}, u32[]{:S(2)}) collective-permute-start(bf16[272,1024]{1,0:T(8,128)(2,1)} %dynamic-slice_bitcast_fusion.9), channel_id=1, source_target_pairs={{0,2},{2,0},{1,3},{3,1},{4,6},{6,4},{5,7},{7,5},{8,10},{10,8},{9,1... | collective-permute-start | bytes 1671176 | tf_op jit(solution)/shard_map/ppermute | solution.py:147
  375.8 26.4 %collective-permute-start.40 = (bf16[272,1088]{1,0:T(8,128)(2,1)S(1)}, bf16[272,1088]{1,0:T(8,128)(2,1)}, u32[]{:S(2)}, u32[]{:S(2)}) collective-permute-start(bf16[272,1088]{1,0:T(8,128)(2,1)S(1)} %dynamic-slice_bitcast_fusion.8), channel_id=1, source_target_pairs={{0,2},{2,0},{1,3},{3,1},{4,6},{6,4},{5,7},{7,5},{8,10},{10,8},{9,1... | collective-permute-start | bytes 1775624 | tf_op jit(solution)/shard_map/ppermute | solution.py:147
  379.2 174.7 %collective-permute-start.47 = (bf16[2,272,4352]{2,1,0:T(8,128)(2,1)}, bf16[2,272,4352]{2,1,0:T(8,128)(2,1)}, u32[]{:S(2)}, u32[]{:S(2)}) collective-permute-start(bf16[2,272,4352]{2,1,0:T(8,128)(2,1)} %dynamic-slice_bitcast_fusion), channel_id=1, source_target_pairs={{0,1},{1,0},{2,3},{3,2},{4,5},{5,4},{6,7},{7,6},{8,9},{9,8},{10,11... | collective-permute-start | bytes 14204936 | tf_op jit(solution)/shard_map/ppermute | solution.py:147
  426.1 97.8 %collective-permute-start.17 = (bf16[2,256,1088]{1,2,0:T(8,128)(2,1)S(1)}, bf16[2,256,1088]{1,2,0:T(8,128)(2,1)S(1)}, u32[]{:S(2)}, u32[]{:S(2)}) collective-permute-start(bf16[2,256,1088]{1,2,0:T(8,128)(2,1)S(1)} %dynamic-slice_bitcast_fusion.6), channel_id=1, source_target_pairs={{0,2},{2,0},{1,3},{3,1},{4,6},{6,4},{5,7},{7,5},{8,10},{10,8},{9,1... | collective-permute-start | bytes 3342344 | tf_op jit(solution)/shard_map/vmap()/ppermute | solution.py:147
  444.2 75.4 %collective-permute-start.30 = (bf16[136,1024]{1,0:T(8,128)(2,1)}, bf16[136,1024]{1,0:T(8,128)(2,1)}, u32[]{:S(2)}, u32[]{:S(2)}) collective-permute-start(bf16[136,1024]{1,0:T(8,128)(2,1)} %pad_maximum_fusion.24), channel_id=1, source_target_pairs={{0,4},{4,0},{1,5},{5,1},{2,6},{6,2},{3,7},{7,3},{8,12},{12,8},{9,1... | collective-permute-start | bytes 835592 | tf_op jit(solution)/shard_map/ppermute | solution.py:103
  448.7 73.0 %collective-permute-start.46 = (bf16[136,1088]{1,0:T(8,128)(2,1)}, bf16[136,1088]{1,0:T(8,128)(2,1)}, u32[]{:S(2)}, u32[]{:S(2)}) collective-permute-start(bf16[136,1088]{1,0:T(8,128)(2,1)} %pad_maximum_fusion.23), channel_id=1, source_target_pairs={{0,4},{4,0},{1,5},{5,1},{2,6},{6,2},{3,7},{7,3},{8,12},{12,8},{9,1... | collective-permute-start | bytes 887816 | tf_op jit(solution)/shard_map/ppermute | solution.py:103
  496.0 69.3 %collective-permute-start.55 = (bf16[2,1088,1088]{2,1,0:T(8,128)(2,1)}, bf16[2,1088,1088]{2,1,0:T(8,128)(2,1)}, u32[]{:S(2)}, u32[]{:S(2)}) collective-permute-start(bf16[2,1088,1088]{2,1,0:T(8,128)(2,1)} %bitcast.359), channel_id=1, source_target_pairs={{0,1},{1,0},{2,3},{3,2},{4,5},{5,4},{6,7},{7,6},{8,9},{9,8},{10,11... | collective-permute-start | bytes 14204936 | tf_op jit(solution)/shard_map/ppermute | solution.py:147
  559.0 83.8 %collective-permute-start.48 = (bf16[272,4352]{1,0:T(8,128)(2,1)}, bf16[272,4352]{1,0:T(8,128)(2,1)}, u32[]{:S(2)}, u32[]{:S(2)}) collective-permute-start(bf16[272,4352]{1,0:T(8,128)(2,1)} %dynamic-slice_bitcast_fusion.3), channel_id=1, source_target_pairs={{0,2},{2,0},{1,3},{3,1},{4,6},{6,4},{5,7},{7,5},{8,10},{10,8},{9,1... | collective-permute-start | bytes 7102472 | tf_op jit(solution)/shard_map/ppermute | solution.py:147
  564.0 76.5 %collective-permute-start.32 = (bf16[272,2240]{1,0:T(8,128)(2,1)}, bf16[272,2240]{1,0:T(8,128)(2,1)}, u32[]{:S(2)}, u32[]{:S(2)}) collective-permute-start(bf16[272,2240]{1,0:T(8,128)(2,1)} %dynamic-slice_bitcast_fusion.5), channel_id=1, source_target_pairs={{0,2},{2,0},{1,3},{3,1},{4,6},{6,4},{5,7},{7,5},{8,10},{10,8},{9,1... | collective-permute-start | bytes 3655688 | tf_op jit(solution)/shard_map/ppermute | solution.py:147
  569.3 119.2 %collective-permute-start.56 = (bf16[1088,1088]{1,0:T(8,128)(2,1)S(1)}, bf16[1088,1088]{1,0:T(8,128)(2,1)S(1)}, u32[]{:S(2)}, u32[]{:S(2)}) collective-permute-start(bf16[1088,1088]{1,0:T(8,128)(2,1)S(1)} %dynamic-slice_bitcast_fusion.1), channel_id=1, source_target_pairs={{0,2},{2,0},{1,3},{3,1},{4,6},{6,4},{5,7},{7,5},{8,10},{10,8},{9,1... | collective-permute-start | bytes 7102472 | tf_op jit(solution)/shard_map/ppermute | solution.py:147
  645.1 56.8 %collective-permute-start.49 = (bf16[136,4352]{1,0:T(8,128)(2,1)S(1)}, bf16[136,4352]{1,0:T(8,128)(2,1)S(1)}, u32[]{:S(2)}, u32[]{:S(2)}) collective-permute-start(bf16[136,4352]{1,0:T(8,128)(2,1)S(1)} %constant_dynamic-slice_fusion.12), channel_id=1, source_target_pairs={{0,4},{4,0},{1,5},{5,1},{2,6},{6,2},{3,7},{7,3},{8,12},{12,8},{9,1... | collective-permute-start | bytes 3551240 | tf_op jit(solution)/shard_map/ppermute | solution.py:97
  659.5 29.7 %collective-permute-start.34 = (bf16[72,2240]{1,0:T(8,128)(2,1)S(1)}, bf16[72,2240]{1,0:T(8,128)(2,1)S(1)}, u32[]{:S(2)}, u32[]{:S(2)}) collective-permute-start(bf16[72,2240]{1,0:T(8,128)(2,1)S(1)} %constant_dynamic-slice_fusion.17), channel_id=1, source_target_pairs={{0,8},{8,0},{16,24},{24,16},{1,9},{9,1},{17,25},{25,17},{2,10},{10... | collective-permute-start | bytes 967688 | tf_op jit(solution)/shard_map/ppermute | solution.py:97
  691.2 25.7 %collective-permute-start.57 = (bf16[544,1088]{1,0:T(8,128)(2,1)S(1)}, bf16[544,1088]{1,0:T(8,128)(2,1)S(1)}, u32[]{:S(2)}, u32[]{:S(2)}) collective-permute-start(bf16[544,1088]{1,0:T(8,128)(2,1)S(1)} %constant_dynamic-slice_fusion.7), channel_id=1, source_target_pairs={{0,4},{4,0},{1,5},{5,1},{2,6},{6,2},{3,7},{7,3},{8,12},{12,8},{9,1... | collective-permute-start | bytes 3551240 | tf_op jit(solution)/shard_map/ppermute | solution.py:97
  702.2 36.4 %collective-permute-start.50 = (bf16[72,4352]{1,0:T(8,128)(2,1)S(1)}, bf16[72,4352]{1,0:T(8,128)(2,1)S(1)}, u32[]{:S(2)}, u32[]{:S(2)}) collective-permute-start(bf16[72,4352]{1,0:T(8,128)(2,1)S(1)} %constant_dynamic-slice_fusion.11), channel_id=1, source_target_pairs={{0,8},{8,0},{16,24},{24,16},{1,9},{9,1},{17,25},{25,17},{2,10},{10... | collective-permute-start | bytes 1880072 | tf_op jit(solution)/shard_map/ppermute | solution.py:97
  727.4 32.2 %collective-permute-start.38 = (bf16[136,2240]{1,0:T(8,128)(2,1)S(1)}, bf16[136,2240]{1,0:T(8,128)(2,1)S(1)}, u32[]{:S(2)}, u32[]{:S(2)}) collective-permute-start(bf16[136,2240]{1,0:T(8,128)(2,1)S(1)} %pad_maximum_fusion.18), channel_id=1, source_target_pairs={{0,4},{4,0},{1,5},{5,1},{2,6},{6,2},{3,7},{7,3},{8,12},{12,8},{9,1... | collective-permute-start | bytes 1827848 | tf_op jit(solution)/shard_map/ppermute | solution.py:103
  738.8 35.2 %collective-permute-start.51 = (bf16[40,4352]{1,0:T(8,128)(2,1)S(1)}, bf16[40,4352]{1,0:T(8,128)(2,1)S(1)}, u32[]{:S(2)}, u32[]{:S(2)}) collective-permute-start(bf16[40,4352]{1,0:T(8,128)(2,1)S(1)} %constant_dynamic-slice_fusion.10), channel_id=1, source_target_pairs={{0,16},{16,0},{8,24},{24,8},{1,17},{17,1},{9,25},{25,9},{2,18},{18... | collective-permute-start | bytes 1044488 | tf_op jit(solution)/shard_map/ppermute | solution.py:97
  759.6 25.0 %collective-permute-start.60 = (bf16[136,1088]{1,0:T(8,128)(2,1)S(1)}, bf16[136,1088]{1,0:T(8,128)(2,1)S(1)}, u32[]{:S(2)}, u32[]{:S(2)}) collective-permute-start(bf16[136,1088]{1,0:T(8,128)(2,1)S(1)} %add_convert_fusion.9), channel_id=1, source_target_pairs={{0,16},{16,0},{8,24},{24,8},{1,17},{17,1},{9,25},{25,9},{2,18},{18... | collective-permute-start | bytes 887816 | tf_op jit(solution)/shard_map/ppermute | solution.py:103
  802.9 30.6 %collective-permute-start.62 = (bf16[544,1088]{1,0:T(8,128)(2,1)S(1)}, bf16[544,1088]{1,0:T(8,128)(2,1)S(1)}, u32[]{:S(2)}, u32[]{:S(2)}) collective-permute-start(bf16[544,1088]{1,0:T(8,128)(2,1)S(1)} %pad_maximum_fusion.11), channel_id=1, source_target_pairs={{0,4},{4,0},{1,5},{5,1},{2,6},{6,2},{3,7},{7,3},{8,12},{12,8},{9,1... | collective-permute-start | bytes 3551240 | tf_op jit(solution)/shard_map/ppermute | solution.py:103
  813.1 38.2 %collective-permute-start.54 = (bf16[136,4352]{1,0:T(8,128)(2,1)S(1)}, bf16[136,4352]{1,0:T(8,128)(2,1)S(1)}, u32[]{:S(2)}, u32[]{:S(2)}) collective-permute-start(bf16[136,4352]{1,0:T(8,128)(2,1)S(1)} %pad_maximum_fusion.14), channel_id=1, source_target_pairs={{0,4},{4,0},{1,5},{5,1},{2,6},{6,2},{3,7},{7,3},{8,12},{12,8},{9,1... | collective-permute-start | bytes 3551240 | tf_op jit(solution)/shard_map/ppermute | solution.py:103
  (156 other events, 1478.5 us)
Sparse Core Ops, SparseCore 0:
  135.7 39.4 all-gather.3

commit v2 on v1

--- a/solution.py
+++ b/solution.py
@@ -4,6 +4,7 @@
 import jax
 import jax.numpy as jnp
 from jax import lax
+from jax.experimental.layout import Layout, with_layout_constraint
 from jax.sharding import PartitionSpec as P
 
 HEADS = 17
@@ -70,19 +71,22 @@
     group = "fsdp"
     sets = "replica"
 
-    def gather(self, shard):
-        return lax.all_gather(shard, "fsdp", axis=0, tiled=True)
-
-    def reduce(self, local):
-        owned = lax.psum_scatter(local, "fsdp", scatter_dimension=0, tiled=True)
-        return lax.psum(owned, "replica").astype(jnp.float32)
+    def gather_all(self, vector, shards):
+        every = lax.all_gather(vector, "fsdp", axis=0)
+        return every, [lax.all_gather(shard, "fsdp", axis=0, tiled=True) for shard in shards]
+
+    def near_sum(self, local):
+        return local
+
+    def group_sum(self, local):
+        return lax.psum_scatter(local, "fsdp", scatter_dimension=0, tiled=True)
+
+    def set_sum(self, owned):
+        return lax.psum(owned, "replica")
 
     def reduce_small(self, packed):
         total = lax.psum(packed, ("replica", "fsdp"))
         return lax.dynamic_index_in_dim(total, lax.axis_index("fsdp"), 0, keepdims=False)
-
-    def scatter_tokens(self, local):
-        return lax.psum_scatter(local, "fsdp", scatter_dimension=1, tiled=True)
 
 
 def split_half(rows):
@@ -106,24 +110,16 @@
     return jnp.concatenate([low[:second], high], axis=0)
 
 
+def add_low(one, two):
+    return (one.astype(jnp.float32) + two.astype(jnp.float32)).astype(one.dtype)
+
+
 class TorusComm:
     group = ("x", "core")
     sets = ("z", "y")
 
-    def gather(self, shard):
-        x, y, core = (lax.axis_index(name) for name in ("x", "y", "core"))
-        rows = shard.shape[0]
-        beside = lax.ppermute(shard, "core", SWAP)
-        if rows % 16 == 0:
-            half = rows // 2
-            piece = lax.dynamic_slice_in_dim(shard, y * half, half, 0)
-            got = lax.ppermute(piece, "x", SWAP)
-            other = lax.ppermute(got, "y", SWAP)
-            far = jnp.concatenate(
-                [jnp.where(y == 0, got, other), jnp.where(y == 0, other, got)], axis=0
-            )
-        else:
-            far = lax.ppermute(shard, "x", SWAP)
+    def finish_gather(self, shard, beside, far):
+        x, core = lax.axis_index("x"), lax.axis_index("core")
         far_beside = lax.ppermute(far, "core", SWAP)
         near_first = jnp.where(core == 0, shard, beside)
         near_second = jnp.where(core == 0, beside, shard)
@@ -139,19 +135,45 @@
             axis=0,
         )
 
-    def scatter_group(self, blocks):
+    def gather_all(self, vector, shards):
+        y = lax.axis_index("y")
+        row = vector.reshape(1, -1)
+        every = self.finish_gather(
+            row, lax.ppermute(row, "core", SWAP), lax.ppermute(row, "x", SWAP)
+        )
+        whole, order = [], every
+        for shard in shards:
+            half = shard.shape[0] // 2
+            beside = lax.ppermute(shard, "core", SWAP)
+            piece = lax.dynamic_slice_in_dim(shard, y * half, half, 0)
+            piece, order = lax.optimization_barrier((piece, order))
+            got = lax.ppermute(piece, "x", SWAP)
+            order = got
+            other = lax.ppermute(got, "y", SWAP)
+            far = jnp.concatenate(
+                [jnp.where(y == 0, got, other), jnp.where(y == 0, other, got)], axis=0
+            )
+            whole.append(self.finish_gather(shard, beside, far))
+        return every, whole
+
+    def near_sum(self, local):
         x, core = lax.axis_index("x"), lax.axis_index("core")
-        for name, place, dim in (("core", core, 1), ("x", x, 0)):
-            keep = lax.dynamic_index_in_dim(blocks, place, dim, keepdims=False)
-            send = lax.dynamic_index_in_dim(blocks, 1 - place, dim, keepdims=False)
-            got = lax.ppermute(send, name, SWAP)
-            blocks = (keep.astype(jnp.float32) + got.astype(jnp.float32)).astype(blocks.dtype)
-        return blocks
-
-    def reduce(self, local):
+        rows = local.shape[0] // 4
+
+        def block(chip, side):
+            return lax.dynamic_slice_in_dim(local, (2 * chip + side) * rows, rows, 0)
+
+        return tuple(
+            add_low(block(chip, core), lax.ppermute(block(chip, 1 - core), "core", SWAP))
+            for chip in (1 - x, x)
+        )
+
+    def group_sum(self, sums):
+        far, near = sums
+        return add_low(near, lax.ppermute(far, "x", SWAP))
+
+    def set_sum(self, own):
         y, z = lax.axis_index("y"), lax.axis_index("z")
-        rows = local.shape[0] // 4
-        own = self.scatter_group(local.reshape(2, 2, rows, local.shape[1]))
         steps = (("y", SWAP, y), ("z", NEAR, lax.rem(z, 2)), ("z", FAR, lax.div(z, 2)))
         sizes = []
         for name, pairs, place in steps:
@@ -159,7 +181,7 @@
             own = halve(own, name, pairs, place)
         for (name, pairs, place), size in zip(steps[::-1], sizes[::-1]):
             own = join(own, name, pairs, place, size)
-        return own.astype(jnp.float32)
+        return own
 
     def reduce_small(self, packed):
         for name, pairs in (
@@ -173,10 +195,12 @@
         place = lax.axis_index("x") * 2 + lax.axis_index("core")
         return lax.dynamic_index_in_dim(packed, place, 0, keepdims=False)
 
-    def scatter_tokens(self, local):
-        sequences, length, width = local.shape
-        blocks = local.reshape(sequences, 2, 2, length // 4, width)
-        return jax.vmap(self.scatter_group)(blocks)
+
+def weight_grad(rows, columns):
+    product = lax.dot_general(
+        rows, columns, (((0,), (0,)), ((), ())), preferred_element_type=jnp.float32
+    ).astype(jnp.bfloat16)
+    return with_layout_constraint(product, Layout(major_to_minor=(0, 1)))
 
 
 def shards(
@@ -209,7 +233,9 @@
         up_bias,
     )
     members = lax.axis_size(comm.group)
-    every = lax.all_gather(jnp.concatenate(vectors), comm.group, axis=0)
+    every, (full_qkv, full_out, full_up, full_down) = comm.gather_all(
+        jnp.concatenate(vectors), (qkv_weight, out_weight, up_weight, down_weight)
+    )
     pieces, position = [], 0
     for member in vectors:
         pieces.append(every[:, position : position + member.size].reshape(-1))
@@ -225,10 +251,6 @@
         down_shift,
         up_shift,
     ) = pieces
-    full_qkv = comm.gather(qkv_weight)
-    full_out = comm.gather(out_weight)
-    full_up = comm.gather(up_weight)
-    full_down = comm.gather(down_weight)
     sequences, local_len, model_width = tokens_in.shape
     row_count = sequences * local_len
     device_index = lax.axis_index(comm.group)
@@ -252,7 +274,7 @@
     )
     key_all, value_all = both_all[0], both_all[1]
     full_len = key_all.shape[1]
-    key_block = min(512, full_len)
+    key_block = min(1024, full_len)
     key_turns = full_len // key_block
     query_heads = queries.reshape(sequences, local_len, HEADS, HEAD_DIM)
     row_index = device_index * local_len + jnp.arange(local_len, dtype=jnp.int32)
@@ -317,19 +339,12 @@
     back_gain_two, back_up, back_down = (second_gain, full_up, full_down)
     upstream = out_grad.reshape(row_count, model_width)
     upstream_full = upstream.astype(jnp.float32)
-    grad_down = comm.reduce(
-        jnp.einsum("rf,rd->fd", hidden, upstream, preferred_element_type=jnp.float32).astype(
-            jnp.bfloat16
-        )
-    )
+    down_near = comm.near_sum(weight_grad(hidden, upstream))
     grad_down_shift = jnp.sum(upstream_full, axis=0)
     hidden_grad = jnp.einsum("rd,fd->rf", upstream, back_down, preferred_element_type=jnp.float32)
+    hidden_grad, down_near = lax.optimization_barrier((hidden_grad, down_near))
     pre_grad = gelu_pull(hidden_grad)[0].astype(jnp.bfloat16)
-    grad_up = comm.reduce(
-        jnp.einsum("rd,rf->df", second_low, pre_grad, preferred_element_type=jnp.float32).astype(
-            jnp.bfloat16
-        )
-    )
+    up_near = comm.near_sum(weight_grad(second_low, pre_grad))
     grad_up_shift = jnp.sum(pre_grad.astype(jnp.float32), axis=0)
     second_grad = jnp.einsum("rf,df->rd", pre_grad, back_up, preferred_element_type=jnp.float32)
     middle_norm_grad, grad_second_gain, grad_second_shift = norm_back(
@@ -337,15 +352,15 @@
     )
     middle_grad = upstream_full + middle_norm_grad
     middle_low = middle_grad.astype(jnp.bfloat16)
-    grad_out = comm.reduce(
-        jnp.einsum("re,rd->ed", attended_low, middle_low, preferred_element_type=jnp.float32).astype(
-            jnp.bfloat16
-        )
-    )
+    out_near = comm.near_sum(weight_grad(attended_low, middle_low))
     grad_out_shift = jnp.sum(middle_low.astype(jnp.float32), axis=0)
     attended_grad = jnp.einsum(
         "rd,ed->re", middle_low, back_out, preferred_element_type=jnp.float32
     ).astype(jnp.bfloat16)
+    attended_grad, up_near, out_near = lax.optimization_barrier(
+        (attended_grad, up_near, out_near)
+    )
+    down_owned = comm.group_sum(down_near)
     grad_heads = attended_grad.reshape(sequences, local_len, HEADS, HEAD_DIM)
     delta_rows = jnp.transpose(
         jnp.sum(grad_heads.astype(jnp.float32) * attended, axis=-1), (0, 2, 1)
@@ -398,19 +413,38 @@
     )
     query_grad, key_grads, value_grads = lax.fori_loop(0, key_turns, backward_step, start_back)
     query_low = query_grad.reshape(row_count, model_width).astype(jnp.bfloat16)
-    own_both = comm.scatter_tokens(
-        jnp.concatenate([key_grads, value_grads], axis=0).astype(jnp.bfloat16)
-    ).reshape(2, row_count, model_width)
-    qkv_grad = jnp.concatenate([query_low, own_both[0], own_both[1]], axis=1)
+    both_grads = jnp.concatenate(
+        [
+            jnp.moveaxis(member.astype(jnp.bfloat16), 0, 1).reshape(full_len, -1)
+            for member in (key_grads, value_grads)
+        ],
+        axis=1,
+    )
+    both_near = comm.near_sum(both_grads)
     early = model_width // 128 * 128
+    early_near = comm.near_sum(weight_grad(normed_low, query_low[:, :early]))
+    both_near, early_near, down_owned = lax.optimization_barrier(
+        (both_near, early_near, down_owned)
+    )
+    own_both = comm.group_sum(both_near)
+    up_owned = comm.group_sum(up_near)
+    own_both, up_owned = lax.optimization_barrier((own_both, up_owned))
+    key_low, value_low = (
+        jnp.moveaxis(member.reshape(local_len, sequences, model_width), 0, 1).reshape(
+            row_count, model_width
+        )
+        for member in jnp.split(own_both, 2, axis=1)
+    )
+    qkv_grad = jnp.concatenate([query_low, key_low, value_low], axis=1)
+    late_near = comm.near_sum(weight_grad(normed_low, qkv_grad[:, early:]))
+    grad_down, grad_up, grad_out = (
+        comm.set_sum(owned).astype(jnp.float32)
+        for owned in (down_owned, up_owned, comm.group_sum(out_near))
+    )
     grad_qkv = jnp.concatenate(
         [
-            comm.reduce(
-                jnp.einsum(
-                    "rd,rc->dc", normed_low, part, preferred_element_type=jnp.float32
-                ).astype(jnp.bfloat16)
-            )
-            for part in (query_low[:, :early], qkv_grad[:, early:])
+            comm.set_sum(comm.group_sum(near)).astype(jnp.float32)
+            for near in (early_near, late_near)
         ],
         axis=1,
     )

time: 874 us -> 681 us (0.78); the launches traced: 861 us -> 677 us
  local copies, waits for them, and re-layouts: 168 us -> 45.6 us
  blocking collectives: 53.8 us -> 0 us
  matrix products: 119 us -> 97.5 us
    unnamed x1 -> x0, blocking collectives: 53.8 us -> none
    dynamic_slice x12 -> x9, local copies, waits for them, and re-layouts: 64.5 us -> 14 us  [the longest x5 9.27 us: block(): return lax.dynamic_slice_in_dim(local, (2 * chip + side) * rows, rows, 0)]
    ppermute x15, waiting for transfers between devices: 94.4 us -> 61.8 us  [join(): got = lax.ppermute(array, name, pairs)]
    unnamed x188 -> x150, local copies, waits for them, and re-layouts: 34.4 us -> 14 us
    ppermute x28 -> x37, waiting for transfers between devices: 159 us -> 179 us  [the longest x6 73.5 us: group_sum(): return add_low(near, lax.ppermute(far, 'x', SWAP))]
    reshape x1, local copies, waits for them, and re-layouts: 16.8 us -> 0.01 us  [gather_all(): row = vector.reshape(1, -1)]
    another operation x7 -> x0, local copies, waits for them, and re-layouts: 12.7 us -> none
    while x66 -> x0, local copies, waits for them, and re-layouts: 9.56 us -> none
  transfers between devices with their start and end apart: 64 -> 73, of which waited for: 31 -> 35; matrix products, arithmetic and copies ran while one was open for 24% -> 29% of each run, Pallas kernels for 0% -> 0%
where the time goes in v2:
time: 681 us; the launch traced here: 677 us
  waiting for transfers between devices  353 us (52%)
  other arithmetic  106 us (16%)
  matrix products  97.5 us (14%)
  starting transfers between devices  60 us (9%)
  local copies, waits for them, and re-layouts  45.6 us (7%)
  between operations  15.8 us (2%)
    ppermute x15, waiting for transfers between devices, halve(): got = lax.ppermute(send, name, pairs)  92 us
    ppermute x6, waiting for transfers between devices, group_sum(): return add_low(near, lax.ppermute(far, 'x', SWAP))  73.5 us
    ppermute x4, waiting for transfers between devices, gather_all(): got = lax.ppermute(piece, 'x', SWAP)  72.5 us
    ppermute x15, waiting for transfers between devices, join(): got = lax.ppermute(array, name, pairs)  61.8 us
    ppermute x4, waiting for transfers between devices, gather_all(): other = lax.ppermute(got, 'y', SWAP)  31 us
    convert_element_type x12, other arithmetic, add_low(): return (one.astype(jnp.float32) + two.astype(jnp.float32)).astype(one.dtype)  28.4 us
    select_n x5, other arithmetic, finish_gather(): jnp.where(x == 0, near_first, far_first)  27.9 us
    ppermute x5, waiting for transfers between devices, reduce_small(): packed = packed + lax.ppermute(packed, name, pairs)  20.1 us
  transfers between devices with their start and end apart: 73, of which 35 were waited for; matrix products, arithmetic and copies ran while one was open for 29% of the time, Pallas kernels for 0%

profile of v2, /device:TPU:0, one launch (start us, length us, event | category | flops | bytes accessed | tf_op | source)
XLA Modules:
  0.0 677.2 jit_solution(10623069214483888865)
XLA Ops:
  7.2 6.3 concatenate.91
  21.8 20.8 %collective-permute-done.4 = bf16[136,3264]{1,0:T(8,128)(2,1)S(1)} collective-permute-done((bf16[136,3264]{1,0:T(8,128)(2,1)S(1)}, bf16[136,3264]{1,0:T(8,128)(2,1)S(1)}, u32[]{:S(2)}, u32[]{:S(2)}) %collective-permute-start.4) | collective-permute-done | bytes 887840 | tf_op jit(solution)/shard_map/ppermute | solution.py:150
  47.2 17.4 %collective-permute-done.5 = bf16[136,3264]{1,0:T(8,128)(2,1)} collective-permute-done((bf16[136,3264]{1,0:T(8,128)(2,1)S(1)}, bf16[136,3264]{1,0:T(8,128)(2,1)}, u32[]{:S(2)}, u32[]{:S(2)}) %collective-permute-start.5) | collective-permute-done | bytes 887840 | tf_op jit(solution)/shard_map/ppermute | solution.py:152
  69.1 8.1 %collective-permute-done.8 = bf16[136,1088]{1,0:T(8,128)(2,1)S(1)} collective-permute-done((bf16[136,1088]{1,0:T(8,128)(2,1)S(1)}, bf16[136,1088]{1,0:T(8,128)(2,1)S(1)}, u32[]{:S(2)}, u32[]{:S(2)}) %collective-permute-start.8) | collective-permute-done | bytes 295968 | tf_op jit(solution)/shard_map/ppermute | solution.py:150
  83.4 21.7 %collective-permute-done.12 = bf16[136,4352]{1,0:T(8,128)(2,1)} collective-permute-done((bf16[136,4352]{1,0:T(8,128)(2,1)}, bf16[136,4352]{1,0:T(8,128)(2,1)}, u32[]{:S(2)}, u32[]{:S(2)}) %collective-permute-start.12) | collective-permute-done | bytes 1183776 | tf_op jit(solution)/shard_map/ppermute | solution.py:150
  120.8 21.9 %collective-permute-done.16 = bf16[544,1088]{1,0:T(8,128)(2,1)} collective-permute-done((bf16[544,1088]{1,0:T(8,128)(2,1)}, bf16[544,1088]{1,0:T(8,128)(2,1)}, u32[]{:S(2)}, u32[]{:S(2)}) %collective-permute-start.16) | collective-permute-done | bytes 1183776 | tf_op jit(solution)/shard_map/ppermute | solution.py:150
  152.0 13.6 %collective-permute-done.17 = bf16[544,1088]{1,0:T(8,128)(2,1)} collective-permute-done((bf16[544,1088]{1,0:T(8,128)(2,1)}, bf16[544,1088]{1,0:T(8,128)(2,1)}, u32[]{:S(2)}, u32[]{:S(2)}) %collective-permute-start.17) | collective-permute-done | bytes 1183776 | tf_op jit(solution)/shard_map/ppermute | solution.py:152
  170.9 8.1 %broadcast_select_fusion.15 = (bf16[272,4352]{1,0:T(8,128)(2,1)}, bf16[272,4352]{1,0:T(8,128)(2,1)}, bf16[272,4352]{1,0:T(8,128)(2,1)}, bf16[272,4352]{1,0:T(8,128)(2,1)}) fusion(pred[]{:T(512)S(6)} %eq.10, bf16[272,4352]{1,0:T(8,128)(2,1)S(1)} %copy-done.26, bf16[272,4352]{1,0:T(8,128)(2,1)} %collective-permute-done.11, pred[]{:T(512)S(6)} %eq.11, ...), kind=kLoop, calls=%fused_computation.72 | loop fusion | flops 14204928 | bytes 18939906 | tf_op jit(solution)/shard_map/jit(_where)/select_n | solution.py:130
  181.9 8.1 %fusion.85 = (f32[17,256]{1,0:T(8,128)S(1)}, f32[17,256,1024]{2,1,0:T(8,128)}) fusion(bf16[256,17,64]{0,2,1:T(8,128)(2,1)S(1)} %bitcast.115, bf16[1024,17,64]{0,2,1:T(8,128)(2,1)S(1)} %bitcast.111, pred[256,1024]{1,0:T(8,128)(4,1)S(1)} %copy-done.52), kind=kOutput, calls=%fused_computation.322 | convolution fusion | flops 583790336 | bytes 20890624 | tf_op jit(solution)/shard_map/while/body/eval_jaxpr/sqhe,skhe->shqk/dot_general | solution.py:43
  190.1 9.6 %fusion = f32[17,256]{1,0:T(8,128)} fusion(f32[17,256,1024]{2,1,0:T(8,128)} %get-tuple-element.223, f32[17,256]{1,0:T(8,128)S(1)} %broadcast_maximum_fusion), kind=kLoop, calls=%fused_computation.6 | loop fusion | flops 8908544 | bytes 17860608 | tf_op jit(solution)/shard_map/while/body/eval_jaxpr/reduce_sum | solution.py:300
  200.5 8.8 %bitcast_convert_fusion = (bf16[1,256,17,64]{1,3,2,0:T(8,128)(2,1)S(1)}, f32[17,256,64]{1,2,0:T(8,128)}) fusion(f32[17,256]{1,0:T(8,128)S(1)} %get-tuple-element.208, bf16[1024,17,64]{0,2,1:T(8,128)(2,1)S(1)} %bitcast.109, f32[17,256,1024]{2,1,0:T(8,128)} %get-tuple-element.223, f32[17,256]{1,0:T(8,128)S(1)} %broadcast_maximum_fusion, ...), kind=kOutput, calls=%fused_computation.147 | convolution fusion | flops 580173824 | bytes 21777408 | tf_op jit(solution)/shard_map/while/body/eval_jaxpr/shqk,skhe->shqe/dot_general | solution.py:301
  212.6 7.7 %multiply_convert_fusion.2 = (bf16[256,4352]{1,0:T(8,128)(2,1)S(1)}, f32[256,4352]{1,0:T(8,128)}) fusion(f32[4352]{0:T(1024)S(1)} %copy-done.66, bf16[272,4352]{1,0:T(8,128)(2,1)} %get-tuple-element.157, bf16[272,4352]{1,0:T(8,128)(2,1)S(1)} %copy-done.35, bf16[272,4352]{1,0:T(8,128)(2,1)S(1)} %copy-done.34, bf16[272,4352]{1,0:T(8,128)(2,1)S(1)} %copy-done.32, ...), kind=kOutput, calls=%fused_computation.37 | convolution fusion | flops 2470264832 | bytes 17296896 | tf_op jit(solution)/shard_map/dot_general | solution.py:327
  232.2 11.9 %broadcast_select_fusion.7 = (bf16[1088,1088]{1,0:T(8,128)(2,1)}, bf16[1088,1088]{1,0:T(8,128)(2,1)}, bf16[1088,1088]{1,0:T(8,128)(2,1)}, bf16[1088,1088]{1,0:T(8,128)(2,1)}) fusion(pred[]{:T(512)S(6)} %eq.10, bf16[1088,1088]{1,0:T(8,128)(2,1)S(1)} %copy-done.25, bf16[1088,1088]{1,0:T(8,128)(2,1)} %collective-permute-done.15, pred[]{:T(512)S(6)} %eq.11, ...), kind=kLoop, calls=%fused_computation.60 | loop fusion | flops 14204928 | bytes 18939906 | tf_op jit(solution)/shard_map/jit(_where)/select_n | solution.py:130
  244.1 9.0 %convolution_bitcast_fusion = f32[256,4352]{1,0:T(8,128)} fusion(bf16[1088,1088]{1,0:T(8,128)(2,1)} %get-tuple-element.149, bf16[1088,1088]{1,0:T(8,128)(2,1)} %get-tuple-element.148, bf16[1088,1088]{1,0:T(8,128)(2,1)} %get-tuple-element.147, bf16[1088,1088]{1,0:T(8,128)(2,1)} %get-tuple-element.146, bf16[1,256,1088]{1,2,0:T(8,128)(2,1)S(1)} %copy-done.39), kind=kOutput, calls=%fused_computation.18 | convolution fusion | flops 2462187520 | bytes 14483456 | tf_op jit(solution)/shard_map/rd,fd->rf/dot_general | solution.py:344
  253.2 7.5 %add_convert_fusion.1 = (bf16[1088,1088]{1,0:T(8,128)(2,1)}, bf16[1088,1088]{1,0:T(8,128)(2,1)}) fusion(bf16[1088,1088]{1,0:T(8,128)(2,1)} %collective-permute-done.20, bf16[4352,1088]{1,0:T(8,128)(2,1)} %copy-done, s32[]{:T(128)S(6)} %select_n.595, bf16[1088,1088]{1,0:T(8,128)(2,1)} %collective-permute-done.19, s32[]{:T(128)S(6)} %select_n.593), kind=kLoop, calls=%fused_computation.29 | loop fusion | flops 9469952 | bytes 14204936 | tf_op jit(solution)/shard_map/convert_element_type | solution.py:114
  263.2 10.6 %multiply_reduce_fusion = (f32[1088]{0:T(1024)S(1)}, f32[256]{0:T(256)S(1)}, f32[256]{0:T(256)S(1)}, f32[1088]{0:T(1024)S(1)}, f32[256,1088]{0,1:T(8,128)S(1)}) fusion(f32[256,1088]{0,1:T(8,128)S(1)} %get-tuple-element.227, f32[256]{0:T(256)S(1)} %add_rsqrt_fusion, f32[256]{0:T(256)S(1)} %broadcast_multiply_fusion.4, f32[1088]{0:T(1024)S(1)} %copy-done.60, ...), kind=kOutput, calls=%fused_computation.149 | convolution fusion | flops 2464691712 | bytes 13943552 | tf_op jit(solution)/shard_map/rf,df->rd/dot_general | solution.py:349
  286.0 7.1 %fusion.12 = bf16[1,256,1088]{1,2,0:T(8,128)(2,1)} fusion(f32[256,1088]{0,1:T(8,128)S(1)} %get-tuple-element.227, bf16[256,4352]{1,0:T(8,128)(2,1)S(1)} %copy-done.30, bf16[1088,1088]{1,0:T(8,128)(2,1)} %get-tuple-element.149, bf16[1088,1088]{1,0:T(8,128)(2,1)} %get-tuple-element.148, bf16[1088,1088]{1,0:T(8,128)(2,1)} %get-tuple-element.147, ...), kind=kOutput, calls=%fused_computation.61 | convolution fusion | flops 2463023104 | bytes 13373696 | tf_op jit(solution)/shard_map/dot_general | solution.py:334
  307.9 9.5 %fusion.13 = bf16[17,64,1024]{2,1,0:T(8,128)(2,1)} fusion(bf16[256,17,64]{0,2,1:T(8,128)(2,1)S(1)} %bitcast.118, f32[17,256,1024]{2,1,0:T(8,128)} %get-tuple-element.223, f32[17,256]{1,0:T(8,128)S(1)} %get-tuple-element.207), kind=kOutput, calls=%fused_computation.76 | convolution fusion | flops 580452352 | bytes 20628480 | tf_op jit(solution)/shard_map/while/body/eval_jaxpr/shqk,sqhe->skhe/dot_general | solution.py:398
  317.4 8.9 %multiply_convert_fusion = bf16[17,256,1024]{2,1,0:T(8,128)(2,1)S(1)} fusion(f32[17,256,1024]{2,1,0:T(8,128)} %get-tuple-element.223, bf16[256,17,64]{0,2,1:T(8,128)(2,1)S(1)} %bitcast.119, bf16[1024,17,64]{0,2,1:T(8,128)(2,1)S(1)} %bitcast.110, f32[17,256]{1,0:T(8,128)S(1)} %bitcast.127, f32[17,256]{1,0:T(8,128)S(1)} %get-tuple-element.207), kind=kOutput, calls=%fused_computation.2 | convolution fusion | flops 588251136 | bytes 29558784 | tf_op jit(solution)/shard_map/while/body/eval_jaxpr/sqhe,skhe->shqk/dot_general | solution.py:63
  335.7 27.7 %collective-permute-done.53 = bf16[272,1088]{1,0:T(8,128)(2,1)S(1)} collective-permute-done((bf16[272,1088]{1,0:T(8,128)(2,1)S(1)}, bf16[272,1088]{1,0:T(8,128)(2,1)S(1)}, u32[]{:S(2)}, u32[]{:S(2)}) %collective-permute-start.53) | collective-permute-done | bytes 591904 | tf_op jit(solution)/shard_map/ppermute | solution.py:173
  400.1 45.7 %collective-permute-done.37 = bf16[272,1024]{1,0:T(8,128)(2,1)S(1)} collective-permute-done((bf16[272,1024]{1,0:T(8,128)(2,1)S(1)}, bf16[272,1024]{1,0:T(8,128)(2,1)S(1)}, u32[]{:S(2)}, u32[]{:S(2)}) %collective-permute-start.37) | collective-permute-done | bytes 557088 | tf_op jit(solution)/shard_map/ppermute | solution.py:173
  448.3 7.3 %collective-permute-done.38 = bf16[136,1024]{1,0:T(8,128)(2,1)S(1)} collective-permute-done((bf16[136,1024]{1,0:T(8,128)(2,1)S(1)}, bf16[136,1024]{1,0:T(8,128)(2,1)S(1)}, u32[]{:S(2)}, u32[]{:S(2)}) %collective-permute-start.38) | collective-permute-done | bytes 278560 | tf_op jit(solution)/shard_map/ppermute | solution.py:101
  498.5 12.1 %collective-permute-done.34 = f32[4,3264]{1,0:T(4,128)S(1)} collective-permute-done((f32[4,3264]{1,0:T(4,128)S(1)}, f32[4,3264]{1,0:T(4,128)S(1)}, u32[]{:S(2)}, u32[]{:S(2)}) %collective-permute-start.34) | collective-permute-done | bytes 52256 | tf_op jit(solution)/shard_map/ppermute | solution.py:194
  524.3 14.5 %collective-permute-done.68 = bf16[136,1088]{1,0:T(8,128)(2,1)S(1)} collective-permute-done((bf16[136,1088]{1,0:T(8,128)(2,1)S(1)}, bf16[136,1088]{1,0:T(8,128)(2,1)S(1)}, u32[]{:S(2)}, u32[]{:S(2)}) %collective-permute-start.68) | collective-permute-done | bytes 295968 | tf_op jit(solution)/shard_map/ppermute | solution.py:101
  539.7 10.0 %collective-permute-done.69 = bf16[136,1088]{1,0:T(8,128)(2,1)S(1)} collective-permute-done((bf16[136,1088]{1,0:T(8,128)(2,1)S(1)}, bf16[136,1088]{1,0:T(8,128)(2,1)S(1)}, u32[]{:S(2)}, u32[]{:S(2)}) %collective-permute-start.69) | collective-permute-done | bytes 295968 | tf_op jit(solution)/shard_map/ppermute | solution.py:107
  556.6 19.0 %collective-permute-done.61 = bf16[72,4352]{1,0:T(8,128)(2,1)S(1)} collective-permute-done((bf16[72,4352]{1,0:T(8,128)(2,1)S(1)}, bf16[72,4352]{1,0:T(8,128)(2,1)S(1)}, u32[]{:S(2)}, u32[]{:S(2)}) %collective-permute-start.61) | collective-permute-done | bytes 626720 | tf_op jit(solution)/shard_map/ppermute | solution.py:101
  578.1 15.0 %collective-permute-done.62 = bf16[40,4352]{1,0:T(8,128)(2,1)S(1)} collective-permute-done((bf16[40,4352]{1,0:T(8,128)(2,1)S(1)}, bf16[40,4352]{1,0:T(8,128)(2,1)S(1)}, u32[]{:S(2)}, u32[]{:S(2)}) %collective-permute-start.62) | collective-permute-done | bytes 348192 | tf_op jit(solution)/shard_map/ppermute | solution.py:101
  595.6 9.0 %collective-permute-done.63 = bf16[40,4352]{1,0:T(8,128)(2,1)S(1)} collective-permute-done((bf16[40,4352]{1,0:T(8,128)(2,1)S(1)}, bf16[40,4352]{1,0:T(8,128)(2,1)S(1)}, u32[]{:S(2)}, u32[]{:S(2)}) %collective-permute-start.63) | collective-permute-done | bytes 348192 | tf_op jit(solution)/shard_map/ppermute | solution.py:107
  611.9 10.1 %collective-permute-done.48 = bf16[72,2240]{1,0:T(8,128)(2,1)S(1)} collective-permute-done((bf16[72,2240]{1,0:T(8,128)(2,1)S(1)}, bf16[72,2240]{1,0:T(8,128)(2,1)S(1)}, u32[]{:S(2)}, u32[]{:S(2)}) %collective-permute-start.48) | collective-permute-done | bytes 322592 | tf_op jit(solution)/shard_map/ppermute | solution.py:101
  622.8 7.9 %collective-permute-done.49 = bf16[40,2240]{1,0:T(8,128)(2,1)S(1)} collective-permute-done((bf16[40,2240]{1,0:T(8,128)(2,1)S(1)}, bf16[40,2240]{1,0:T(8,128)(2,1)S(1)}, u32[]{:S(2)}, u32[]{:S(2)}) %collective-permute-start.49) | collective-permute-done | bytes 179232 | tf_op jit(solution)/shard_map/ppermute | solution.py:101
  631.0 6.8 %collective-permute-done.50 = bf16[40,2240]{1,0:T(8,128)(2,1)S(1)} collective-permute-done((bf16[40,2240]{1,0:T(8,128)(2,1)S(1)}, bf16[40,2240]{1,0:T(8,128)(2,1)S(1)}, u32[]{:S(2)}, u32[]{:S(2)}) %collective-permute-start.50) | collective-permute-done | bytes 179232 | tf_op jit(solution)/shard_map/ppermute | solution.py:107
  646.3 14.9 %collective-permute-done.65 = bf16[136,4352]{1,0:T(8,128)(2,1)S(1)} collective-permute-done((bf16[136,4352]{1,0:T(8,128)(2,1)S(1)}, bf16[136,4352]{1,0:T(8,128)(2,1)S(1)}, u32[]{:S(2)}, u32[]{:S(2)}) %collective-permute-start.65) | collective-permute-done | bytes 1183776 | tf_op jit(solution)/shard_map/ppermute | solution.py:107
  (443 shorter events, 244.7 us)
Async XLA Ops:
  7.2 171.8 %all-gather.3.cloned.1.call-start = ((), (), s32[]{:S(2)}) async-start(), calls=%async_computation | async-start | bytes 5570560 | tf_op jit(solution)/shard_map/all_gather | solution.py:269
  19.7 22.8 %collective-permute-start.4 = (bf16[136,3264]{1,0:T(8,128)(2,1)S(1)}, bf16[136,3264]{1,0:T(8,128)(2,1)S(1)}, u32[]{:S(2)}, u32[]{:S(2)}) collective-permute-start(bf16[136,3264]{1,0:T(8,128)(2,1)S(1)} %constant_dynamic-slice_fusion.30), channel_id=1, source_target_pairs={{0,2},{2,0},{1,3},{3,1},{4,6},{6,4},{5,7},{7,5},{8,10},{10,8},{9,1... | collective-permute-start | bytes 2663432 | tf_op jit(solution)/shard_map/ppermute | solution.py:150
  44.3 62.4 %collective-permute-start.3 = (bf16[272,3264]{1,0:T(8,128)(2,1)}, bf16[272,3264]{1,0:T(8,128)(2,1)}, u32[]{:S(2)}, u32[]{:S(2)}) collective-permute-start(bf16[272,3264]{1,0:T(8,128)(2,1)} %param.18), channel_id=1, source_target_pairs={{0,1},{1,0},{2,3},{3,2},{4,5},{5,4},{6,7},{7,6},{8,9},{9,8},{10,11... | collective-permute-start | bytes 5326856 | tf_op jit(solution)/shard_map/ppermute | solution.py:147
  44.3 103.4 %collective-permute-start.7 = (bf16[272,1088]{1,0:T(8,128)(2,1)}, bf16[272,1088]{1,0:T(8,128)(2,1)}, u32[]{:S(2)}, u32[]{:S(2)}) collective-permute-start(bf16[272,1088]{1,0:T(8,128)(2,1)} %param.21), channel_id=1, source_target_pairs={{0,1},{1,0},{2,3},{3,2},{4,5},{5,4},{6,7},{7,6},{8,9},{9,8},{10,11... | collective-permute-start | bytes 1775624 | tf_op jit(solution)/shard_map/ppermute | solution.py:147
  44.8 124.7 %collective-permute-start.11 = (bf16[272,4352]{1,0:T(8,128)(2,1)}, bf16[272,4352]{1,0:T(8,128)(2,1)}, u32[]{:S(2)}, u32[]{:S(2)}) collective-permute-start(bf16[272,4352]{1,0:T(8,128)(2,1)} %param.25), channel_id=1, source_target_pairs={{0,1},{1,0},{2,3},{3,2},{4,5},{5,4},{6,7},{7,6},{8,9},{9,8},{10,11... | collective-permute-start | bytes 7102472 | tf_op jit(solution)/shard_map/ppermute | solution.py:147
  67.2 41.0 %collective-permute-start.6 = (bf16[272,3264]{1,0:T(8,128)(2,1)}, bf16[272,3264]{1,0:T(8,128)(2,1)}, u32[]{:S(2)}, u32[]{:S(2)}) collective-permute-start(bf16[272,3264]{1,0:T(8,128)(2,1)} %pad_maximum_fusion.6), channel_id=1, source_target_pairs={{0,1},{1,0},{2,3},{3,2},{4,5},{5,4},{6,7},{7,6},{8,9},{9,8},{10,11... | collective-permute-start | bytes 5326856 | tf_op jit(solution)/shard_map/ppermute | solution.py:123
  77.1 28.0 %collective-permute-start.12 = (bf16[136,4352]{1,0:T(8,128)(2,1)}, bf16[136,4352]{1,0:T(8,128)(2,1)}, u32[]{:S(2)}, u32[]{:S(2)}) collective-permute-start(bf16[136,4352]{1,0:T(8,128)(2,1)} %constant_dynamic-slice_fusion.28), channel_id=1, source_target_pairs={{0,2},{2,0},{1,3},{3,1},{4,6},{6,4},{5,7},{7,5},{8,10},{10,8},{9,1... | collective-permute-start | bytes 3551240 | tf_op jit(solution)/shard_map/ppermute | solution.py:150
  106.7 36.0 %collective-permute-start.16 = (bf16[544,1088]{1,0:T(8,128)(2,1)}, bf16[544,1088]{1,0:T(8,128)(2,1)}, u32[]{:S(2)}, u32[]{:S(2)}) collective-permute-start(bf16[544,1088]{1,0:T(8,128)(2,1)} %constant_dynamic-slice_fusion.27), channel_id=1, source_target_pairs={{0,2},{2,0},{1,3},{3,1},{4,6},{6,4},{5,7},{7,5},{8,10},{10,8},{9,1... | collective-permute-start | bytes 3551240 | tf_op jit(solution)/shard_map/ppermute | solution.py:150
  108.2 34.5 %collective-permute-start.13 = (bf16[136,4352]{1,0:T(8,128)(2,1)}, bf16[136,4352]{1,0:T(8,128)(2,1)}, u32[]{:S(2)}, u32[]{:S(2)}) collective-permute-start(bf16[136,4352]{1,0:T(8,128)(2,1)} %collective-permute-done.12), channel_id=1, source_target_pairs={{0,4},{4,0},{1,5},{5,1},{2,6},{6,2},{3,7},{7,3},{8,12},{12,8},{9,1... | collective-permute-start | bytes 3551240 | tf_op jit(solution)/shard_map/ppermute | solution.py:152
  120.8 27.4 %collective-permute-start.10 = (bf16[272,1088]{1,0:T(8,128)(2,1)}, bf16[272,1088]{1,0:T(8,128)(2,1)}, u32[]{:S(2)}, u32[]{:S(2)}) collective-permute-start(bf16[272,1088]{1,0:T(8,128)(2,1)} %pad_maximum_fusion.17), channel_id=1, source_target_pairs={{0,1},{1,0},{2,3},{3,2},{4,5},{5,4},{6,7},{7,6},{8,9},{9,8},{10,11... | collective-permute-start | bytes 1775624 | tf_op jit(solution)/shard_map/ppermute | solution.py:123
  142.7 22.9 %collective-permute-start.17 = (bf16[544,1088]{1,0:T(8,128)(2,1)}, bf16[544,1088]{1,0:T(8,128)(2,1)}, u32[]{:S(2)}, u32[]{:S(2)}) collective-permute-start(bf16[544,1088]{1,0:T(8,128)(2,1)} %collective-permute-done.16), channel_id=1, source_target_pairs={{0,4},{4,0},{1,5},{5,1},{2,6},{6,2},{3,7},{7,3},{8,12},{12,8},{9,1... | collective-permute-start | bytes 3551240 | tf_op jit(solution)/shard_map/ppermute | solution.py:152
  146.3 23.1 %collective-permute-start.14 = (bf16[272,4352]{1,0:T(8,128)(2,1)}, bf16[272,4352]{1,0:T(8,128)(2,1)}, u32[]{:S(2)}, u32[]{:S(2)}) collective-permute-start(bf16[272,4352]{1,0:T(8,128)(2,1)} %pad_maximum_fusion.5), channel_id=1, source_target_pairs={{0,1},{1,0},{2,3},{3,2},{4,5},{5,4},{6,7},{7,6},{8,9},{9,8},{10,11... | collective-permute-start | bytes 7102472 | tf_op jit(solution)/shard_map/ppermute | solution.py:123
  147.7 84.5 %collective-permute-start.15 = (bf16[1088,1088]{1,0:T(8,128)(2,1)}, bf16[1088,1088]{1,0:T(8,128)(2,1)}, u32[]{:S(2)}, u32[]{:S(2)}) collective-permute-start(bf16[1088,1088]{1,0:T(8,128)(2,1)} %param.27), channel_id=1, source_target_pairs={{0,1},{1,0},{2,3},{3,2},{4,5},{5,4},{6,7},{7,6},{8,9},{9,8},{10,11... | collective-permute-start | bytes 7102472 | tf_op jit(solution)/shard_map/ppermute | solution.py:147
  169.5 62.7 %collective-permute-start.18 = (bf16[1088,1088]{1,0:T(8,128)(2,1)}, bf16[1088,1088]{1,0:T(8,128)(2,1)}, u32[]{:S(2)}, u32[]{:S(2)}) collective-permute-start(bf16[1088,1088]{1,0:T(8,128)(2,1)} %pad_maximum_fusion.4), channel_id=1, source_target_pairs={{0,1},{1,0},{2,3},{3,2},{4,5},{5,4},{6,7},{7,6},{8,9},{9,8},{10,11... | collective-permute-start | bytes 7102472 | tf_op jit(solution)/shard_map/ppermute | solution.py:123
  293.2 79.4 %collective-permute-start.29 = (bf16[1088,1088]{1,0:T(8,128)(2,1)}, bf16[1088,1088]{1,0:T(8,128)(2,1)}, u32[]{:S(2)}, u32[]{:S(2)}) collective-permute-start(bf16[1088,1088]{1,0:T(8,128)(2,1)} %get-tuple-element.110), channel_id=1, source_target_pairs={{0,2},{2,0},{1,3},{3,1},{4,6},{6,4},{5,7},{7,5},{8,10},{10,8},{9,1... | collective-permute-start | bytes 7102472 | tf_op jit(solution)/shard_map/ppermute | solution.py:173
  332.3 31.2 %collective-permute-start.53 = (bf16[272,1088]{1,0:T(8,128)(2,1)S(1)}, bf16[272,1088]{1,0:T(8,128)(2,1)S(1)}, u32[]{:S(2)}, u32[]{:S(2)}) collective-permute-start(bf16[272,1088]{1,0:T(8,128)(2,1)S(1)} %copy-done.57), channel_id=1, source_target_pairs={{0,2},{2,0},{1,3},{3,1},{4,6},{6,4},{5,7},{7,5},{8,10},{10,8},{9,1... | collective-permute-start | bytes 1775624 | tf_op jit(solution)/shard_map/ppermute | solution.py:173
  333.5 47.4 %collective-permute-start.27 = (bf16[272,1024]{1,0:T(8,128)(2,1)}, bf16[272,1024]{1,0:T(8,128)(2,1)}, u32[]{:S(2)}, u32[]{:S(2)}) collective-permute-start(bf16[272,1024]{1,0:T(8,128)(2,1)} %get-tuple-element.191), channel_id=1, source_target_pairs={{0,1},{1,0},{2,3},{3,2},{4,5},{5,4},{6,7},{7,6},{8,9},{9,8},{10,11... | collective-permute-start | bytes 1671176 | tf_op jit(solution)/shard_map/ppermute | solution.py:167
  334.0 49.4 %collective-permute-start.28 = (bf16[272,1024]{1,0:T(8,128)(2,1)}, bf16[272,1024]{1,0:T(8,128)(2,1)}, u32[]{:S(2)}, u32[]{:S(2)}) collective-permute-start(bf16[272,1024]{1,0:T(8,128)(2,1)} %get-tuple-element.190), channel_id=1, source_target_pairs={{0,1},{1,0},{2,3},{3,2},{4,5},{5,4},{6,7},{7,6},{8,9},{9,8},{10,11... | collective-permute-start | bytes 1671176 | tf_op jit(solution)/shard_map/ppermute | solution.py:167
  379.4 98.2 %collective-permute-start.31 = (bf16[272,4352]{1,0:T(8,128)(2,1)}, bf16[272,4352]{1,0:T(8,128)(2,1)S(1)}, u32[]{:S(2)}, u32[]{:S(2)}) collective-permute-start(bf16[272,4352]{1,0:T(8,128)(2,1)} %get-tuple-element.114), channel_id=1, source_target_pairs={{0,2},{2,0},{1,3},{3,1},{4,6},{6,4},{5,7},{7,5},{8,10},{10,8},{9,1... | collective-permute-start | bytes 7102472 | tf_op jit(solution)/shard_map/ppermute | solution.py:173
  391.5 54.3 %collective-permute-start.37 = (bf16[272,1024]{1,0:T(8,128)(2,1)S(1)}, bf16[272,1024]{1,0:T(8,128)(2,1)S(1)}, u32[]{:S(2)}, u32[]{:S(2)}) collective-permute-start(bf16[272,1024]{1,0:T(8,128)(2,1)S(1)} %get-tuple-element.117), channel_id=1, source_target_pairs={{0,2},{2,0},{1,3},{3,1},{4,6},{6,4},{5,7},{7,5},{8,10},{10,8},{9,1... | collective-permute-start | bytes 1671176 | tf_op jit(solution)/shard_map/ppermute | solution.py:173
  395.3 80.4 %collective-permute-start.66 = (bf16[544,1088]{1,0:T(8,128)(2,1)S(1)}, bf16[544,1088]{1,0:T(8,128)(2,1)S(1)}, u32[]{:S(2)}, u32[]{:S(2)}) collective-permute-start(bf16[544,1088]{1,0:T(8,128)(2,1)S(1)} %constant_dynamic-slice_fusion.2), channel_id=1, source_target_pairs={{0,4},{4,0},{1,5},{5,1},{2,6},{6,2},{3,7},{7,3},{8,12},{12,8},{9,1... | collective-permute-start | bytes 3551240 | tf_op jit(solution)/shard_map/ppermute | solution.py:101
  396.4 72.8 %collective-permute-start.30 = (bf16[256,2176]{0,1:T(8,128)(2,1)S(1)}, bf16[256,2176]{0,1:T(8,128)(2,1)S(1)}, u32[]{:S(2)}, u32[]{:S(2)}) collective-permute-start(bf16[256,2176]{0,1:T(8,128)(2,1)S(1)} %get-tuple-element.112), channel_id=1, source_target_pairs={{0,2},{2,0},{1,3},{3,1},{4,6},{6,4},{5,7},{7,5},{8,10},{10,8},{9,1... | collective-permute-start | bytes 3342344 | tf_op jit(solution)/shard_map/ppermute | solution.py:173
  476.9 38.7 %collective-permute-start.67 = (bf16[272,1088]{1,0:T(8,128)(2,1)}, bf16[272,1088]{1,0:T(8,128)(2,1)}, u32[]{:S(2)}, u32[]{:S(2)}) collective-permute-start(bf16[272,1088]{1,0:T(8,128)(2,1)} %constant_dynamic-slice_fusion.1), channel_id=1, source_target_pairs={{0,8},{8,0},{16,24},{24,16},{1,9},{9,1},{17,25},{25,17},{2,10},{10... | collective-permute-start | bytes 1775624 | tf_op jit(solution)/shard_map/ppermute | solution.py:101
  486.7 63.2 %collective-permute-start.60 = (bf16[136,4352]{1,0:T(8,128)(2,1)}, bf16[136,4352]{1,0:T(8,128)(2,1)}, u32[]{:S(2)}, u32[]{:S(2)}) collective-permute-start(bf16[136,4352]{1,0:T(8,128)(2,1)} %constant_dynamic-slice_fusion.5), channel_id=1, source_target_pairs={{0,4},{4,0},{1,5},{5,1},{2,6},{6,2},{3,7},{7,3},{8,12},{12,8},{9,1... | collective-permute-start | bytes 3551240 | tf_op jit(solution)/shard_map/ppermute | solution.py:101
  488.9 64.7 %collective-permute-start.45 = (bf16[272,2240]{1,0:T(8,128)(2,1)}, bf16[272,2240]{1,0:T(8,128)(2,1)}, u32[]{:S(2)}, u32[]{:S(2)}) collective-permute-start(bf16[272,2240]{1,0:T(8,128)(2,1)} %get-tuple-element.163), channel_id=1, source_target_pairs={{0,1},{1,0},{2,3},{3,2},{4,5},{5,4},{6,7},{7,6},{8,9},{9,8},{10,11... | collective-permute-start | bytes 3655688 | tf_op jit(solution)/shard_map/ppermute | solution.py:167
  492.7 100.6 %collective-permute-start.44 = (bf16[272,2240]{1,0:T(8,128)(2,1)S(1)}, bf16[272,2240]{1,0:T(8,128)(2,1)S(1)}, u32[]{:S(2)}, u32[]{:S(2)}) collective-permute-start(bf16[272,2240]{1,0:T(8,128)(2,1)S(1)} %copy-done.51), channel_id=1, source_target_pairs={{0,1},{1,0},{2,3},{3,2},{4,5},{5,4},{6,7},{7,6},{8,9},{9,8},{10,11... | collective-permute-start | bytes 3655688 | tf_op jit(solution)/shard_map/ppermute | solution.py:167
  514.8 24.8 %collective-permute-start.43 = (bf16[136,1024]{1,0:T(8,128)(2,1)S(1)}, bf16[136,1024]{1,0:T(8,128)(2,1)S(1)}, u32[]{:S(2)}, u32[]{:S(2)}) collective-permute-start(bf16[136,1024]{1,0:T(8,128)(2,1)S(1)} %pad_maximum_fusion.24), channel_id=1, source_target_pairs={{0,4},{4,0},{1,5},{5,1},{2,6},{6,2},{3,7},{7,3},{8,12},{12,8},{9,1... | collective-permute-start | bytes 835592 | tf_op jit(solution)/shard_map/ppermute | solution.py:107
  549.8 26.7 %collective-permute-start.70 = (bf16[272,1088]{1,0:T(8,128)(2,1)S(1)}, bf16[272,1088]{1,0:T(8,128)(2,1)S(1)}, u32[]{:S(2)}, u32[]{:S(2)}) collective-permute-start(bf16[272,1088]{1,0:T(8,128)(2,1)S(1)} %pad_maximum_fusion.19), channel_id=1, source_target_pairs={{0,8},{8,0},{16,24},{24,16},{1,9},{9,1},{17,25},{25,17},{2,10},{10... | collective-permute-start | bytes 1775624 | tf_op jit(solution)/shard_map/ppermute | solution.py:107
  551.6 24.0 %collective-permute-start.61 = (bf16[72,4352]{1,0:T(8,128)(2,1)S(1)}, bf16[72,4352]{1,0:T(8,128)(2,1)S(1)}, u32[]{:S(2)}, u32[]{:S(2)}) collective-permute-start(bf16[72,4352]{1,0:T(8,128)(2,1)S(1)} %constant_dynamic-slice_fusion.4), channel_id=1, source_target_pairs={{0,8},{8,0},{16,24},{24,16},{1,9},{9,1},{17,25},{25,17},{2,10},{10... | collective-permute-start | bytes 1880072 | tf_op jit(solution)/shard_map/ppermute | solution.py:101
  555.3 37.9 %collective-permute-start.46 = (bf16[272,2240]{1,0:T(8,128)(2,1)S(1)}, bf16[272,2240]{1,0:T(8,128)(2,1)S(1)}, u32[]{:S(2)}, u32[]{:S(2)}) collective-permute-start(bf16[272,2240]{1,0:T(8,128)(2,1)S(1)} %add_convert_fusion.9), channel_id=1, source_target_pairs={{0,2},{2,0},{1,3},{3,1},{4,6},{6,4},{5,7},{7,5},{8,10},{10,8},{9,1... | collective-permute-start | bytes 3655688 | tf_op jit(solution)/shard_map/ppermute | solution.py:173
  576.8 28.0 %collective-permute-start.71 = (bf16[544,1088]{1,0:T(8,128)(2,1)S(1)}, bf16[544,1088]{1,0:T(8,128)(2,1)S(1)}, u32[]{:S(2)}, u32[]{:S(2)}) collective-permute-start(bf16[544,1088]{1,0:T(8,128)(2,1)S(1)} %pad_maximum_fusion.11), channel_id=1, source_target_pairs={{0,4},{4,0},{1,5},{5,1},{2,6},{6,2},{3,7},{7,3},{8,12},{12,8},{9,1... | collective-permute-start | bytes 3551240 | tf_op jit(solution)/shard_map/ppermute | solution.py:107
  638.0 23.2 %collective-permute-start.65 = (bf16[136,4352]{1,0:T(8,128)(2,1)S(1)}, bf16[136,4352]{1,0:T(8,128)(2,1)S(1)}, u32[]{:S(2)}, u32[]{:S(2)}) collective-permute-start(bf16[136,4352]{1,0:T(8,128)(2,1)S(1)} %pad_maximum_fusion.14), channel_id=1, source_target_pairs={{0,4},{4,0},{1,5},{5,1},{2,6},{6,2},{3,7},{7,3},{8,12},{12,8},{9,1... | collective-permute-start | bytes 3551240 | tf_op jit(solution)/shard_map/ppermute | solution.py:107
  (116 other events, 1122.4 us)
Sparse Core Ops, SparseCore 0:
  119.0 42.0 all-gather.2

commit v3 on v2

--- a/solution.py
+++ b/solution.py
@@ -71,9 +71,11 @@
     group = "fsdp"
     sets = "replica"
 
-    def gather_all(self, vector, shards):
-        every = lax.all_gather(vector, "fsdp", axis=0)
-        return every, [lax.all_gather(shard, "fsdp", axis=0, tiled=True) for shard in shards]
+    def gather_vectors(self, vector):
+        return lax.all_gather(vector, "fsdp", axis=0)
+
+    def gather(self, shard, order):
+        return lax.all_gather(shard, "fsdp", axis=0, tiled=True), order
 
     def near_sum(self, local):
         return local
@@ -81,8 +83,11 @@
     def group_sum(self, local):
         return lax.psum_scatter(local, "fsdp", scatter_dimension=0, tiled=True)
 
-    def set_sum(self, owned):
+    def set_share(self, owned):
         return lax.psum(owned, "replica")
+
+    def set_join(self, share, rows):
+        return share
 
     def reduce_small(self, packed):
         total = lax.psum(packed, ("replica", "fsdp"))
@@ -135,26 +140,24 @@
             axis=0,
         )
 
-    def gather_all(self, vector, shards):
+    def gather_vectors(self, vector):
+        row = vector.reshape(1, -1)
+        return self.finish_gather(
+            row, lax.ppermute(row, "core", SWAP), lax.ppermute(row, "x", SWAP)
+        )
+
+    def gather(self, shard, order):
         y = lax.axis_index("y")
-        row = vector.reshape(1, -1)
-        every = self.finish_gather(
-            row, lax.ppermute(row, "core", SWAP), lax.ppermute(row, "x", SWAP)
-        )
-        whole, order = [], every
-        for shard in shards:
-            half = shard.shape[0] // 2
-            beside = lax.ppermute(shard, "core", SWAP)
-            piece = lax.dynamic_slice_in_dim(shard, y * half, half, 0)
-            piece, order = lax.optimization_barrier((piece, order))
-            got = lax.ppermute(piece, "x", SWAP)
-            order = got
-            other = lax.ppermute(got, "y", SWAP)
-            far = jnp.concatenate(
-                [jnp.where(y == 0, got, other), jnp.where(y == 0, other, got)], axis=0
-            )
-            whole.append(self.finish_gather(shard, beside, far))
-        return every, whole
+        half = shard.shape[0] // 2
+        beside = lax.ppermute(shard, "core", SWAP)
+        piece = lax.dynamic_slice_in_dim(shard, y * half, half, 0)
+        piece, _ = lax.optimization_barrier((piece, order))
+        got = lax.ppermute(piece, "x", SWAP)
+        other = lax.ppermute(got, "y", SWAP)
+        far = jnp.concatenate(
+            [jnp.where(y == 0, got, other), jnp.where(y == 0, other, got)], axis=0
+        )
+        return self.finish_gather(shard, beside, far), got
 
     def near_sum(self, local):
         x, core = lax.axis_index("x"), lax.axis_index("core")
@@ -172,16 +175,22 @@
         far, near = sums
         return add_low(near, lax.ppermute(far, "x", SWAP))
 
-    def set_sum(self, own):
+    def set_steps(self):
         y, z = lax.axis_index("y"), lax.axis_index("z")
-        steps = (("y", SWAP, y), ("z", NEAR, lax.rem(z, 2)), ("z", FAR, lax.div(z, 2)))
-        sizes = []
-        for name, pairs, place in steps:
-            sizes.append(own.shape[0])
+        return (("y", SWAP, y), ("z", NEAR, lax.rem(z, 2)), ("z", FAR, lax.div(z, 2)))
+
+    def set_share(self, own):
+        for name, pairs, place in self.set_steps():
             own = halve(own, name, pairs, place)
-        for (name, pairs, place), size in zip(steps[::-1], sizes[::-1]):
-            own = join(own, name, pairs, place, size)
         return own
+
+    def set_join(self, share, rows):
+        sizes = [rows]
+        for _ in range(2):
+            sizes.append(split_half(sizes[-1])[0])
+        for (name, pairs, place), size in zip(self.set_steps()[::-1], sizes[::-1]):
+            share = join(share, name, pairs, place, size)
+        return share
 
     def reduce_small(self, packed):
         for name, pairs in (
@@ -233,9 +242,10 @@
         up_bias,
     )
     members = lax.axis_size(comm.group)
-    every, (full_qkv, full_out, full_up, full_down) = comm.gather_all(
-        jnp.concatenate(vectors), (qkv_weight, out_weight, up_weight, down_weight)
-    )
+    every = comm.gather_vectors(jnp.concatenate(vectors))
+    full_qkv, order = comm.gather(qkv_weight, every)
+    full_out, _ = comm.gather(out_weight, order)
+    full_up, _ = comm.gather(up_weight, order)
     pieces, position = [], 0
     for member in vectors:
         pieces.append(every[:, position : position + member.size].reshape(-1))
@@ -273,6 +283,7 @@
         tiled=True,
     )
     key_all, value_all = both_all[0], both_all[1]
+    full_down, _ = comm.gather(down_weight, both_all)
     full_len = key_all.shape[1]
     key_block = min(1024, full_len)
     key_turns = full_len // key_block
@@ -343,6 +354,7 @@
     grad_down_shift = jnp.sum(upstream_full, axis=0)
     hidden_grad = jnp.einsum("rd,fd->rf", upstream, back_down, preferred_element_type=jnp.float32)
     hidden_grad, down_near = lax.optimization_barrier((hidden_grad, down_near))
+    down_owned = comm.group_sum(down_near)
     pre_grad = gelu_pull(hidden_grad)[0].astype(jnp.bfloat16)
     up_near = comm.near_sum(weight_grad(second_low, pre_grad))
     grad_up_shift = jnp.sum(pre_grad.astype(jnp.float32), axis=0)
@@ -360,7 +372,7 @@
     attended_grad, up_near, out_near = lax.optimization_barrier(
         (attended_grad, up_near, out_near)
     )
-    down_owned = comm.group_sum(down_near)
+    up_owned = comm.group_sum(up_near)
     grad_heads = attended_grad.reshape(sequences, local_len, HEADS, HEAD_DIM)
     delta_rows = jnp.transpose(
         jnp.sum(grad_heads.astype(jnp.float32) * attended, axis=-1), (0, 2, 1)
@@ -412,6 +424,10 @@
         jnp.zeros((sequences, full_len, model_width), jnp.float32),
     )
     query_grad, key_grads, value_grads = lax.fori_loop(0, key_turns, backward_step, start_back)
+    query_grad, key_grads, value_grads, down_owned = lax.optimization_barrier(
+        (query_grad, key_grads, value_grads, down_owned)
+    )
+    down_share = comm.set_share(down_owned)
     query_low = query_grad.reshape(row_count, model_width).astype(jnp.bfloat16)
     both_grads = jnp.concatenate(
         [
@@ -423,12 +439,16 @@
     both_near = comm.near_sum(both_grads)
     early = model_width // 128 * 128
     early_near = comm.near_sum(weight_grad(normed_low, query_low[:, :early]))
-    both_near, early_near, down_owned = lax.optimization_barrier(
-        (both_near, early_near, down_owned)
+    both_near, early_near, up_owned, out_near = lax.optimization_barrier(
+        (both_near, early_near, up_owned, out_near)
     )
     own_both = comm.group_sum(both_near)
-    up_owned = comm.group_sum(up_near)
-    own_both, up_owned = lax.optimization_barrier((own_both, up_owned))
+    up_share = comm.set_share(up_owned)
+    own_both, down_share, early_near, out_near = lax.optimization_barrier(
+        (own_both, down_share, early_near, out_near)
+    )
+    out_owned = comm.group_sum(out_near)
+    early_owned = comm.group_sum(early_near)
     key_low, value_low = (
         jnp.moveaxis(member.reshape(local_len, sequences, model_width), 0, 1).reshape(
             row_count, model_width
@@ -437,17 +457,23 @@
     )
     qkv_grad = jnp.concatenate([query_low, key_low, value_low], axis=1)
     late_near = comm.near_sum(weight_grad(normed_low, qkv_grad[:, early:]))
-    grad_down, grad_up, grad_out = (
-        comm.set_sum(owned).astype(jnp.float32)
-        for owned in (down_owned, up_owned, comm.group_sum(out_near))
-    )
-    grad_qkv = jnp.concatenate(
-        [
-            comm.set_sum(comm.group_sum(near)).astype(jnp.float32)
-            for near in (early_near, late_near)
-        ],
-        axis=1,
-    )
+    late_near, up_share = lax.optimization_barrier((late_near, up_share))
+    late_owned = comm.group_sum(late_near)
+    out_share, early_share, late_share = (
+        comm.set_share(owned) for owned in (out_owned, early_owned, late_owned)
+    )
+    down_sum, up_sum, out_sum, early_sum, late_sum = (
+        comm.set_join(share, owner.shape[0]).astype(jnp.float32)
+        for share, owner in (
+            (down_share, down_weight),
+            (up_share, up_weight),
+            (out_share, out_weight),
+            (early_share, qkv_weight),
+            (late_share, qkv_weight),
+        )
+    )
+    grad_down, grad_up, grad_out = down_sum, up_sum, out_sum
+    grad_qkv = jnp.concatenate([early_sum, late_sum], axis=1)
     grad_query_shift = jnp.sum(qkv_grad[:, :model_width].astype(jnp.float32), axis=0)
     grad_value_shift = jnp.sum(qkv_grad[:, 2 * model_width :].astype(jnp.float32), axis=0)
     first_grad = jnp.einsum("rc,dc->rd", qkv_grad, back_qkv, preferred_element_type=jnp.float32)

time: 681 us -> 662 us (0.972)
  waiting for transfers between devices: 353 us -> 308 us
  local copies, waits for them, and re-layouts: 45.6 us -> 54 us
  other arithmetic: 106 us -> 114 us
  starting transfers between devices: 60 us -> 67.2 us
    ppermute x15, waiting for transfers between devices: 92 us -> 63.7 us  [halve(): got = lax.ppermute(send, name, pairs)]
    ppermute x14, waiting for transfers between devices: 105 us -> 119 us  [the longest x4 64.1 us: gather(): other = lax.ppermute(got, 'y', SWAP)]
    ppermute x6, waiting for transfers between devices: 73.5 us -> 61.7 us  [group_sum(): return add_low(near, lax.ppermute(far, 'x', SWAP))]
    ppermute x15, starting transfers between devices: 9.77 us -> 20.3 us  [join(): got = lax.ppermute(array, name, pairs)]
    ppermute x15, waiting for transfers between devices: 61.8 us -> 52.2 us  [join(): got = lax.ppermute(array, name, pairs)]
    ppermute x5, waiting for transfers between devices: 20.1 us -> 11 us  [reduce_small(): packed = packed + lax.ppermute(packed, name, pairs)]
    unnamed x150 -> x182, local copies, waits for them, and re-layouts: 14 us -> 20.1 us
  transfers between devices with their start and end apart: 73 -> 73, of which waited for: 35 -> 33; matrix products, arithmetic and copies ran while one was open for 29% -> 33% of each run, Pallas kernels for 0% -> 0%
where the time goes in v3:
time: 662 us; the launch traced here: 658 us
  waiting for transfers between devices  308 us (47%)
  other arithmetic  114 us (17%)
  matrix products  99.1 us (15%)
  starting transfers between devices  67.2 us (10%)
  local copies, waits for them, and re-layouts  54 us (8%)
  between operations  15.9 us (2%)
    ppermute x4, waiting for transfers between devices, gather(): other = lax.ppermute(got, 'y', SWAP)  64.1 us
    ppermute x15, waiting for transfers between devices, halve(): got = lax.ppermute(send, name, pairs)  63.7 us
    ppermute x6, waiting for transfers between devices, group_sum(): return add_low(near, lax.ppermute(far, 'x', SWAP))  61.7 us
    ppermute x4, waiting for transfers between devices, gather(): got = lax.ppermute(piece, 'x', SWAP)  53.5 us
    ppermute x15, waiting for transfers between devices, join(): got = lax.ppermute(array, name, pairs)  52.2 us
    convert_element_type x12, other arithmetic, add_low(): return (one.astype(jnp.float32) + two.astype(jnp.float32)).astype(one.dtype)  34 us
    select_n x5, other arithmetic, finish_gather(): jnp.where(x == 0, near_first, far_first)  28 us
    ppermute x15, starting transfers between devices, join(): got = lax.ppermute(array, name, pairs)  20.3 us
  transfers between devices with their start and end apart: 73, of which 33 were waited for; matrix products, arithmetic and copies ran while one was open for 33% of the time, Pallas kernels for 0%

profile of v3, /device:TPU:0, one launch (start us, length us, event | category | flops | bytes accessed | tf_op | source)
XLA Modules:
  0.0 658.3 jit_solution(12804946405245963029)
XLA Ops:
  7.2 6.3 concatenate.91
  21.8 20.8 %collective-permute-done.4 = bf16[136,3264]{1,0:T(8,128)(2,1)S(1)} collective-permute-done((bf16[136,3264]{1,0:T(8,128)(2,1)S(1)}, bf16[136,3264]{1,0:T(8,128)(2,1)S(1)}, u32[]{:S(2)}, u32[]{:S(2)}) %collective-permute-start.4) | collective-permute-done | bytes 887840 | tf_op jit(solution)/shard_map/ppermute | solution.py:155
  48.4 16.1 %collective-permute-done.5 = bf16[136,3264]{1,0:T(8,128)(2,1)} collective-permute-done((bf16[136,3264]{1,0:T(8,128)(2,1)S(1)}, bf16[136,3264]{1,0:T(8,128)(2,1)}, u32[]{:S(2)}, u32[]{:S(2)}) %collective-permute-start.5) | collective-permute-done | bytes 887840 | tf_op jit(solution)/shard_map/ppermute | solution.py:156
  77.4 31.6 %collective-permute-done.8 = bf16[136,1088]{1,0:T(8,128)(2,1)S(1)} collective-permute-done((bf16[136,1088]{1,0:T(8,128)(2,1)}, bf16[136,1088]{1,0:T(8,128)(2,1)S(1)}, u32[]{:S(2)}, u32[]{:S(2)}) %collective-permute-start.8) | collective-permute-done | bytes 295968 | tf_op jit(solution)/shard_map/ppermute | solution.py:155
  121.4 25.0 %collective-permute-done.9 = bf16[136,1088]{1,0:T(8,128)(2,1)} collective-permute-done((bf16[136,1088]{1,0:T(8,128)(2,1)S(1)}, bf16[136,1088]{1,0:T(8,128)(2,1)}, u32[]{:S(2)}, u32[]{:S(2)}) %collective-permute-start.9) | collective-permute-done | bytes 295968 | tf_op jit(solution)/shard_map/ppermute | solution.py:156
  148.3 23.0 %collective-permute-done.13 = bf16[136,4352]{1,0:T(8,128)(2,1)} collective-permute-done((bf16[136,4352]{1,0:T(8,128)(2,1)}, bf16[136,4352]{1,0:T(8,128)(2,1)}, u32[]{:S(2)}, u32[]{:S(2)}) %collective-permute-start.13) | collective-permute-done | bytes 1183776 | tf_op jit(solution)/shard_map/ppermute | solution.py:156
  185.2 8.2 %broadcast_select_fusion.15 = (bf16[272,4352]{1,0:T(8,128)(2,1)}, bf16[272,4352]{1,0:T(8,128)(2,1)}, bf16[272,4352]{1,0:T(8,128)(2,1)}, bf16[272,4352]{1,0:T(8,128)(2,1)}) fusion(pred[]{:T(512)S(6)} %eq.10, bf16[272,4352]{1,0:T(8,128)(2,1)S(1)} %copy-done.29, bf16[272,4352]{1,0:T(8,128)(2,1)} %collective-permute-done.11, pred[]{:T(512)S(6)} %eq.11, ...), kind=kLoop, calls=%fused_computation.71 | loop fusion | flops 14204928 | bytes 18939906 | tf_op jit(solution)/shard_map/jit(_where)/select_n | solution.py:135
  196.3 8.1 %fusion.82 = (f32[17,256]{1,0:T(8,128)S(1)}, f32[17,256,1024]{2,1,0:T(8,128)}) fusion(bf16[256,17,64]{0,2,1:T(8,128)(2,1)S(1)} %bitcast.123, bf16[1024,17,64]{0,2,1:T(8,128)(2,1)S(1)} %bitcast.119, pred[256,1024]{1,0:T(8,128)(4,1)S(1)} %copy-done.62), kind=kOutput, calls=%fused_computation.323 | convolution fusion | flops 583790336 | bytes 20890624 | tf_op jit(solution)/shard_map/while/body/eval_jaxpr/sqhe,skhe->shqk/dot_general | solution.py:43
  204.4 9.6 %fusion = f32[17,256]{1,0:T(8,128)} fusion(f32[17,256,1024]{2,1,0:T(8,128)} %get-tuple-element.251, f32[17,256]{1,0:T(8,128)S(1)} %broadcast_maximum_fusion), kind=kLoop, calls=%fused_computation.6 | loop fusion | flops 8908544 | bytes 17860608 | tf_op jit(solution)/shard_map/while/body/eval_jaxpr/reduce_sum | solution.py:311
  214.8 8.8 %bitcast_convert_fusion = (bf16[1,256,17,64]{1,3,2,0:T(8,128)(2,1)S(1)}, f32[17,256,64]{1,2,0:T(8,128)}) fusion(f32[17,256]{1,0:T(8,128)S(1)} %get-tuple-element.236, bf16[1024,17,64]{0,2,1:T(8,128)(2,1)S(1)} %bitcast.117, f32[17,256,1024]{2,1,0:T(8,128)} %get-tuple-element.251, f32[17,256]{1,0:T(8,128)S(1)} %broadcast_maximum_fusion, ...), kind=kOutput, calls=%fused_computation.148 | convolution fusion | flops 580173824 | bytes 21777408 | tf_op jit(solution)/shard_map/while/body/eval_jaxpr/shqk,skhe->shqe/dot_general | solution.py:312
  227.3 7.7 %multiply_convert_fusion.1 = (bf16[256,4352]{1,0:T(8,128)(2,1)S(1)}, f32[256,4352]{1,0:T(8,128)}) fusion(f32[4352]{0:T(1024)S(1)} %copy-done.78, bf16[272,4352]{1,0:T(8,128)(2,1)} %get-tuple-element.183, bf16[272,4352]{1,0:T(8,128)(2,1)S(1)} %copy-done.46, bf16[272,4352]{1,0:T(8,128)(2,1)S(1)} %copy-done.44, bf16[272,4352]{1,0:T(8,128)(2,1)S(1)} %copy-done.42, ...), kind=kOutput, calls=%fused_computation.36 | convolution fusion | flops 2470264832 | bytes 17296896 | tf_op jit(solution)/shard_map/dot_general | solution.py:338
  246.8 11.9 %broadcast_select_fusion.7 = (bf16[1088,1088]{1,0:T(8,128)(2,1)}, bf16[1088,1088]{1,0:T(8,128)(2,1)}, bf16[1088,1088]{1,0:T(8,128)(2,1)}, bf16[1088,1088]{1,0:T(8,128)(2,1)}) fusion(pred[]{:T(512)S(6)} %eq.10, bf16[1088,1088]{1,0:T(8,128)(2,1)S(1)} %copy-done.27, bf16[1088,1088]{1,0:T(8,128)(2,1)} %collective-permute-done.15, pred[]{:T(512)S(6)} %eq.11, ...), kind=kLoop, calls=%fused_computation.59 | loop fusion | flops 14204928 | bytes 18939906 | tf_op jit(solution)/shard_map/jit(_where)/select_n | solution.py:135
  258.7 9.0 %convolution_bitcast_fusion = f32[256,4352]{1,0:T(8,128)} fusion(bf16[1088,1088]{1,0:T(8,128)(2,1)} %get-tuple-element.175, bf16[1088,1088]{1,0:T(8,128)(2,1)} %get-tuple-element.174, bf16[1088,1088]{1,0:T(8,128)(2,1)} %get-tuple-element.173, bf16[1088,1088]{1,0:T(8,128)(2,1)} %get-tuple-element.172, bf16[1,256,1088]{1,2,0:T(8,128)(2,1)S(1)} %copy-done.48), kind=kOutput, calls=%fused_computation.18 | convolution fusion | flops 2462187520 | bytes 14483456 | tf_op jit(solution)/shard_map/rd,fd->rf/dot_general | solution.py:355
  267.8 7.5 %add_convert_fusion.1 = (bf16[1088,1088]{1,0:T(8,128)(2,1)}, bf16[1088,1088]{1,0:T(8,128)(2,1)}) fusion(bf16[1088,1088]{1,0:T(8,128)(2,1)} %collective-permute-done.20, bf16[4352,1088]{1,0:T(8,128)(2,1)} %copy-done, s32[]{:T(128)S(6)} %select_n.595, bf16[1088,1088]{1,0:T(8,128)(2,1)} %collective-permute-done.19, s32[]{:T(128)S(6)} %select_n.593), kind=kLoop, calls=%fused_computation.29 | loop fusion | flops 9469952 | bytes 14204936 | tf_op jit(solution)/shard_map/convert_element_type | solution.py:119
  288.4 9.4 %multiply_reduce_fusion = (f32[1088]{0:T(1024)S(1)}, f32[256]{0:T(256)S(1)}, f32[256]{0:T(256)S(1)}, f32[1088]{0:T(1024)S(1)}, f32[256,1088]{0,1:T(8,128)S(1)}) fusion(f32[256,1088]{0,1:T(8,128)S(1)} %get-tuple-element.255, f32[256]{0:T(256)S(1)} %add_rsqrt_fusion, f32[256]{0:T(256)S(1)} %broadcast_multiply_fusion.5, f32[1088]{0:T(1024)S(1)} %copy-done.71, ...), kind=kOutput, calls=%fused_computation.150 | convolution fusion | flops 2464691712 | bytes 13943552 | tf_op jit(solution)/shard_map/rf,df->rd/dot_general | solution.py:361
  309.9 7.2 %add_convert_fusion.4 = (bf16[272,4352]{1,0:T(8,128)(2,1)}, bf16[272,4352]{1,0:T(8,128)(2,1)}) fusion(bf16[272,4352]{1,0:T(8,128)(2,1)} %collective-permute-done.22, bf16[1088,4352]{1,0:T(8,128)(2,1)} %copy-done.1, s32[]{:T(128)S(6)} %select_n.599, bf16[272,4352]{1,0:T(8,128)(2,1)} %collective-permute-done.21, s32[]{:T(128)S(6)} %select_n.597), kind=kLoop, calls=%fused_computation.32 | loop fusion | flops 9469952 | bytes 14204936 | tf_op jit(solution)/shard_map/convert_element_type | solution.py:119
  317.4 10.9 %multiply_convert_fusion = bf16[17,256,1024]{2,1,0:T(8,128)(2,1)} fusion(f32[17,256,1024]{2,1,0:T(8,128)} %get-tuple-element.251, bf16[256,17,64]{0,2,1:T(8,128)(2,1)S(1)} %bitcast.126, bf16[1024,17,64]{0,2,1:T(8,128)(2,1)S(1)} %bitcast.118, f32[17,256]{1,0:T(8,128)S(1)} %bitcast.135, f32[17,256]{1,0:T(8,128)S(1)} %get-tuple-element.235), kind=kOutput, calls=%fused_computation.2 | convolution fusion | flops 588251136 | bytes 29558784 | tf_op jit(solution)/shard_map/while/body/eval_jaxpr/sqhe,skhe->shqk/dot_general | solution.py:63
  328.3 6.7 %broadcast_multiply_fusion = bf16[17,64,1024]{2,1,0:T(8,128)(2,1)} fusion(bf16[256,17,64]{0,2,1:T(8,128)(2,1)S(1)} %bitcast.124, bf16[17,256,1024]{2,1,0:T(8,128)(2,1)} %multiply_convert_fusion), kind=kOutput, calls=%fused_computation.77 | convolution fusion | flops 572653568 | bytes 11698176 | tf_op jit(solution)/shard_map/while/body/eval_jaxpr/shqk,sqhe->skhe/dot_general | solution.py:405
  335.0 7.2 %fusion.19 = bf16[1,256,17,64]{1,3,2,0:T(8,128)(2,1)S(1)} fusion(bf16[1024,17,64]{0,2,1:T(8,128)(2,1)S(1)} %bitcast.120, bf16[17,256,1024]{2,1,0:T(8,128)(2,1)} %multiply_convert_fusion), kind=kOutput, calls=%fused_computation.99 | convolution fusion | flops 570982400 | bytes 11698176 | tf_op jit(solution)/shard_map/while/body/eval_jaxpr/shqk,skhe->sqhe/dot_general | solution.py:399
  346.7 13.0 %collective-permute-done.25 = bf16[1088,1088]{1,0:T(8,128)(2,1)} collective-permute-done((bf16[1088,1088]{1,0:T(8,128)(2,1)}, bf16[1088,1088]{1,0:T(8,128)(2,1)}, u32[]{:S(2)}, u32[]{:S(2)}) %collective-permute-start.25) | collective-permute-done | bytes 2367520 | tf_op jit(solution)/shard_map/ppermute | solution.py:176
  382.9 10.2 %collective-permute-done.32 = bf16[544,1088]{1,0:T(8,128)(2,1)} collective-permute-done((bf16[544,1088]{1,0:T(8,128)(2,1)}, bf16[544,1088]{1,0:T(8,128)(2,1)}, u32[]{:S(2)}, u32[]{:S(2)}) %collective-permute-start.32) | collective-permute-done | bytes 1183776 | tf_op jit(solution)/shard_map/ppermute | solution.py:106
  400.1 8.9 %collective-permute-done.33 = bf16[272,1088]{1,0:T(8,128)(2,1)S(1)} collective-permute-done((bf16[272,1088]{1,0:T(8,128)(2,1)S(1)}, bf16[272,1088]{1,0:T(8,128)(2,1)S(1)}, u32[]{:S(2)}, u32[]{:S(2)}) %collective-permute-start.33) | collective-permute-done | bytes 591904 | tf_op jit(solution)/shard_map/ppermute | solution.py:106
  412.6 18.5 %collective-permute-done.30 = bf16[272,4352]{1,0:T(8,128)(2,1)S(1)} collective-permute-done((bf16[272,4352]{1,0:T(8,128)(2,1)}, bf16[272,4352]{1,0:T(8,128)(2,1)S(1)}, u32[]{:S(2)}, u32[]{:S(2)}) %collective-permute-start.30) | collective-permute-done | bytes 2367520 | tf_op jit(solution)/shard_map/ppermute | solution.py:176
  438.8 19.3 %collective-permute-done.31 = bf16[256,2176]{0,1:T(8,128)(2,1)} collective-permute-done((bf16[256,2176]{0,1:T(8,128)(2,1)}, bf16[256,2176]{0,1:T(8,128)(2,1)}, u32[]{:S(2)}, u32[]{:S(2)}) %collective-permute-start.31) | collective-permute-done | bytes 1114144 | tf_op jit(solution)/shard_map/ppermute | solution.py:176
  497.1 11.0 %collective-permute-done.40 = bf16[272,1024]{1,0:T(8,128)(2,1)S(1)} collective-permute-done((bf16[272,1024]{1,0:T(8,128)(2,1)S(1)}, bf16[272,1024]{1,0:T(8,128)(2,1)S(1)}, u32[]{:S(2)}, u32[]{:S(2)}) %collective-permute-start.40) | collective-permute-done | bytes 557088 | tf_op jit(solution)/shard_map/ppermute | solution.py:176
  511.8 6.5 collective-permute-done.41
  519.5 9.8 %collective-permute-done.70 = bf16[272,1088]{1,0:T(8,128)(2,1)S(1)} collective-permute-done((bf16[272,1088]{1,0:T(8,128)(2,1)S(1)}, bf16[272,1088]{1,0:T(8,128)(2,1)S(1)}, u32[]{:S(2)}, u32[]{:S(2)}) %collective-permute-start.70) | collective-permute-done | bytes 591904 | tf_op jit(solution)/shard_map/ppermute | solution.py:112
  535.7 6.7 %collective-permute-done.61 = bf16[72,1088]{1,0:T(8,128)(2,1)S(1)} collective-permute-done((bf16[72,1088]{1,0:T(8,128)(2,1)S(1)}, bf16[72,1088]{1,0:T(8,128)(2,1)S(1)}, u32[]{:S(2)}, u32[]{:S(2)}) %collective-permute-start.61) | collective-permute-done | bytes 156704 | tf_op jit(solution)/shard_map/ppermute | solution.py:106
  552.3 7.3 %collective-permute-done.44 = bf16[40,1024]{1,0:T(8,128)(2,1)S(1)} collective-permute-done((bf16[40,1024]{1,0:T(8,128)(2,1)S(1)}, bf16[40,1024]{1,0:T(8,128)(2,1)S(1)}, u32[]{:S(2)}, u32[]{:S(2)}) %collective-permute-start.44) | collective-permute-done | bytes 81952 | tf_op jit(solution)/shard_map/ppermute | solution.py:112
  599.5 6.9 %collective-permute-done.54 = bf16[72,2240]{1,0:T(8,128)(2,1)S(1)} collective-permute-done((bf16[72,2240]{1,0:T(8,128)(2,1)S(1)}, bf16[72,2240]{1,0:T(8,128)(2,1)S(1)}, u32[]{:S(2)}, u32[]{:S(2)}) %collective-permute-start.54) | collective-permute-done | bytes 322592 | tf_op jit(solution)/shard_map/ppermute | solution.py:106
  607.3 7.7 %collective-permute-done.55 = bf16[40,2240]{1,0:T(8,128)(2,1)S(1)} collective-permute-done((bf16[40,2240]{1,0:T(8,128)(2,1)S(1)}, bf16[40,2240]{1,0:T(8,128)(2,1)S(1)}, u32[]{:S(2)}, u32[]{:S(2)}) %collective-permute-start.55) | collective-permute-done | bytes 179232 | tf_op jit(solution)/shard_map/ppermute | solution.py:106
  622.4 15.4 %collective-permute-done.68 = bf16[136,4352]{1,0:T(8,128)(2,1)S(1)} collective-permute-done((bf16[136,4352]{1,0:T(8,128)(2,1)S(1)}, bf16[136,4352]{1,0:T(8,128)(2,1)S(1)}, u32[]{:S(2)}, u32[]{:S(2)}) %collective-permute-start.68) | collective-permute-done | bytes 1183776 | tf_op jit(solution)/shard_map/ppermute | solution.py:112
  (477 shorter events, 266.1 us)
Async XLA Ops:
  7.2 186.2 %all-gather.3.cloned.1.call-start = ((), (), s32[]{:S(2)}) async-start(), calls=%async_computation | async-start | bytes 5570560 | tf_op jit(solution)/shard_map/all_gather | solution.py:279
  19.7 22.8 %collective-permute-start.4 = (bf16[136,3264]{1,0:T(8,128)(2,1)S(1)}, bf16[136,3264]{1,0:T(8,128)(2,1)S(1)}, u32[]{:S(2)}, u32[]{:S(2)}) collective-permute-start(bf16[136,3264]{1,0:T(8,128)(2,1)S(1)} %constant_dynamic-slice_fusion.30), channel_id=1, source_target_pairs={{0,2},{2,0},{1,3},{3,1},{4,6},{6,4},{5,7},{7,5},{8,10},{10,8},{9,1... | collective-permute-start | bytes 2663432 | tf_op jit(solution)/shard_map/ppermute | solution.py:155
  44.3 64.7 %collective-permute-start.3 = (bf16[272,3264]{1,0:T(8,128)(2,1)}, bf16[272,3264]{1,0:T(8,128)(2,1)}, u32[]{:S(2)}, u32[]{:S(2)}) collective-permute-start(bf16[272,3264]{1,0:T(8,128)(2,1)} %param.18), channel_id=1, source_target_pairs={{0,1},{1,0},{2,3},{3,2},{4,5},{5,4},{6,7},{7,6},{8,9},{9,8},{10,11... | collective-permute-start | bytes 5326856 | tf_op jit(solution)/shard_map/ppermute | solution.py:152
  46.7 30.7 %collective-permute-start.16 = (bf16[544,1088]{1,0:T(8,128)(2,1)}, bf16[544,1088]{1,0:T(8,128)(2,1)}, u32[]{:S(2)}, u32[]{:S(2)}) collective-permute-start(bf16[544,1088]{1,0:T(8,128)(2,1)} %constant_dynamic-slice_fusion.27), channel_id=1, source_target_pairs={{0,2},{2,0},{1,3},{3,1},{4,6},{6,4},{5,7},{7,5},{8,10},{10,8},{9,1... | collective-permute-start | bytes 3551240 | tf_op jit(solution)/shard_map/ppermute | solution.py:155
  67.2 43.8 %collective-permute-start.6 = (bf16[272,3264]{1,0:T(8,128)(2,1)}, bf16[272,3264]{1,0:T(8,128)(2,1)}, u32[]{:S(2)}, u32[]{:S(2)}) collective-permute-start(bf16[272,3264]{1,0:T(8,128)(2,1)} %pad_maximum_fusion.6), channel_id=1, source_target_pairs={{0,1},{1,0},{2,3},{3,2},{4,5},{5,4},{6,7},{7,6},{8,9},{9,8},{10,11... | collective-permute-start | bytes 5326856 | tf_op jit(solution)/shard_map/ppermute | solution.py:128
  69.3 40.0 %collective-permute-start.12 = (bf16[136,4352]{1,0:T(8,128)(2,1)}, bf16[136,4352]{1,0:T(8,128)(2,1)}, u32[]{:S(2)}, u32[]{:S(2)}) collective-permute-start(bf16[136,4352]{1,0:T(8,128)(2,1)} %constant_dynamic-slice_fusion.28), channel_id=1, source_target_pairs={{0,2},{2,0},{1,3},{3,1},{4,6},{6,4},{5,7},{7,5},{8,10},{10,8},{9,1... | collective-permute-start | bytes 3551240 | tf_op jit(solution)/shard_map/ppermute | solution.py:155
  72.7 36.3 %collective-permute-start.8 = (bf16[136,1088]{1,0:T(8,128)(2,1)}, bf16[136,1088]{1,0:T(8,128)(2,1)S(1)}, u32[]{:S(2)}, u32[]{:S(2)}) collective-permute-start(bf16[136,1088]{1,0:T(8,128)(2,1)} %constant_dynamic-slice_fusion.29), channel_id=1, source_target_pairs={{0,2},{2,0},{1,3},{3,1},{4,6},{6,4},{5,7},{7,5},{8,10},{10,8},{9,1... | collective-permute-start | bytes 887816 | tf_op jit(solution)/shard_map/ppermute | solution.py:155
  77.4 98.2 %collective-permute-start.7 = (bf16[272,1088]{1,0:T(8,128)(2,1)S(1)}, bf16[272,1088]{1,0:T(8,128)(2,1)}, u32[]{:S(2)}, u32[]{:S(2)}) collective-permute-start(bf16[272,1088]{1,0:T(8,128)(2,1)S(1)} %copy-done.61), channel_id=1, source_target_pairs={{0,1},{1,0},{2,3},{3,2},{4,5},{5,4},{6,7},{7,6},{8,9},{9,8},{10,11... | collective-permute-start | bytes 1775624 | tf_op jit(solution)/shard_map/ppermute | solution.py:152
  109.0 74.8 %collective-permute-start.11 = (bf16[272,4352]{1,0:T(8,128)(2,1)}, bf16[272,4352]{1,0:T(8,128)(2,1)}, u32[]{:S(2)}, u32[]{:S(2)}) collective-permute-start(bf16[272,4352]{1,0:T(8,128)(2,1)} %param.25), channel_id=1, source_target_pairs={{0,1},{1,0},{2,3},{3,2},{4,5},{5,4},{6,7},{7,6},{8,9},{9,8},{10,11... | collective-permute-start | bytes 7102472 | tf_op jit(solution)/shard_map/ppermute | solution.py:152
  109.0 70.9 %collective-permute-start.17 = (bf16[544,1088]{1,0:T(8,128)(2,1)}, bf16[544,1088]{1,0:T(8,128)(2,1)}, u32[]{:S(2)}, u32[]{:S(2)}) collective-permute-start(bf16[544,1088]{1,0:T(8,128)(2,1)} %collective-permute-done.16), channel_id=1, source_target_pairs={{0,4},{4,0},{1,5},{5,1},{2,6},{6,2},{3,7},{7,3},{8,12},{12,8},{9,1... | collective-permute-start | bytes 3551240 | tf_op jit(solution)/shard_map/ppermute | solution.py:156
  109.2 37.1 %collective-permute-start.9 = (bf16[136,1088]{1,0:T(8,128)(2,1)S(1)}, bf16[136,1088]{1,0:T(8,128)(2,1)}, u32[]{:S(2)}, u32[]{:S(2)}) collective-permute-start(bf16[136,1088]{1,0:T(8,128)(2,1)S(1)} %collective-permute-done.8), channel_id=1, source_target_pairs={{0,4},{4,0},{1,5},{5,1},{2,6},{6,2},{3,7},{7,3},{8,12},{12,8},{9,1... | collective-permute-start | bytes 887816 | tf_op jit(solution)/shard_map/ppermute | solution.py:156
  111.0 60.3 %collective-permute-start.13 = (bf16[136,4352]{1,0:T(8,128)(2,1)}, bf16[136,4352]{1,0:T(8,128)(2,1)}, u32[]{:S(2)}, u32[]{:S(2)}) collective-permute-start(bf16[136,4352]{1,0:T(8,128)(2,1)} %collective-permute-done.12), channel_id=1, source_target_pairs={{0,4},{4,0},{1,5},{5,1},{2,6},{6,2},{3,7},{7,3},{8,12},{12,8},{9,1... | collective-permute-start | bytes 3551240 | tf_op jit(solution)/shard_map/ppermute | solution.py:156
  148.3 27.8 %collective-permute-start.10 = (bf16[272,1088]{1,0:T(8,128)(2,1)}, bf16[272,1088]{1,0:T(8,128)(2,1)}, u32[]{:S(2)}, u32[]{:S(2)}) collective-permute-start(bf16[272,1088]{1,0:T(8,128)(2,1)} %pad_maximum_fusion.17), channel_id=1, source_target_pairs={{0,1},{1,0},{2,3},{3,2},{4,5},{5,4},{6,7},{7,6},{8,9},{9,8},{10,11... | collective-permute-start | bytes 1775624 | tf_op jit(solution)/shard_map/ppermute | solution.py:128
  175.6 71.2 %collective-permute-start.15 = (bf16[1088,1088]{1,0:T(8,128)(2,1)}, bf16[1088,1088]{1,0:T(8,128)(2,1)}, u32[]{:S(2)}, u32[]{:S(2)}) collective-permute-start(bf16[1088,1088]{1,0:T(8,128)(2,1)} %param.27), channel_id=1, source_target_pairs={{0,1},{1,0},{2,3},{3,2},{4,5},{5,4},{6,7},{7,6},{8,9},{9,8},{10,11... | collective-permute-start | bytes 7102472 | tf_op jit(solution)/shard_map/ppermute | solution.py:152
  183.7 63.1 %collective-permute-start.18 = (bf16[1088,1088]{1,0:T(8,128)(2,1)}, bf16[1088,1088]{1,0:T(8,128)(2,1)}, u32[]{:S(2)}, u32[]{:S(2)}) collective-permute-start(bf16[1088,1088]{1,0:T(8,128)(2,1)} %pad_maximum_fusion.4), channel_id=1, source_target_pairs={{0,1},{1,0},{2,3},{3,2},{4,5},{5,4},{6,7},{7,6},{8,9},{9,8},{10,11... | collective-permute-start | bytes 7102472 | tf_op jit(solution)/shard_map/ppermute | solution.py:128
  287.9 22.1 %collective-permute-start.21 = (bf16[272,4352]{1,0:T(8,128)(2,1)}, bf16[272,4352]{1,0:T(8,128)(2,1)}, u32[]{:S(2)}, u32[]{:S(2)}) collective-permute-start(bf16[272,4352]{1,0:T(8,128)(2,1)} %get-tuple-element.179), channel_id=1, source_target_pairs={{0,1},{1,0},{2,3},{3,2},{4,5},{5,4},{6,7},{7,6},{8,9},{9,8},{10,11... | collective-permute-start | bytes 7102472 | tf_op jit(solution)/shard_map/ppermute | solution.py:170
  287.9 22.0 %collective-permute-start.22 = (bf16[272,4352]{1,0:T(8,128)(2,1)}, bf16[272,4352]{1,0:T(8,128)(2,1)}, u32[]{:S(2)}, u32[]{:S(2)}) collective-permute-start(bf16[272,4352]{1,0:T(8,128)(2,1)} %get-tuple-element.178), channel_id=1, source_target_pairs={{0,1},{1,0},{2,3},{3,2},{4,5},{5,4},{6,7},{7,6},{8,9},{9,8},{10,11... | collective-permute-start | bytes 7102472 | tf_op jit(solution)/shard_map/ppermute | solution.py:170
  303.0 56.7 %collective-permute-start.25 = (bf16[1088,1088]{1,0:T(8,128)(2,1)}, bf16[1088,1088]{1,0:T(8,128)(2,1)}, u32[]{:S(2)}, u32[]{:S(2)}) collective-permute-start(bf16[1088,1088]{1,0:T(8,128)(2,1)} %get-tuple-element.123), channel_id=1, source_target_pairs={{0,2},{2,0},{1,3},{3,1},{4,6},{6,4},{5,7},{7,5},{8,10},{10,8},{9,1... | collective-permute-start | bytes 7102472 | tf_op jit(solution)/shard_map/ppermute | solution.py:176
  364.1 28.9 %collective-permute-start.32 = (bf16[544,1088]{1,0:T(8,128)(2,1)}, bf16[544,1088]{1,0:T(8,128)(2,1)}, u32[]{:S(2)}, u32[]{:S(2)}) collective-permute-start(bf16[544,1088]{1,0:T(8,128)(2,1)} %constant_dynamic-slice_fusion.17), channel_id=1, source_target_pairs={{0,4},{4,0},{1,5},{5,1},{2,6},{6,2},{3,7},{7,3},{8,12},{12,8},{9,1... | collective-permute-start | bytes 3551240 | tf_op jit(solution)/shard_map/ppermute | solution.py:106
  370.4 25.9 %collective-permute-start.26 = (bf16[256,2176]{0,1:T(8,128)(2,1)}, bf16[256,2176]{0,1:T(8,128)(2,1)}, u32[]{:S(2)}, u32[]{:S(2)}) collective-permute-start(bf16[256,2176]{0,1:T(8,128)(2,1)} %get-tuple-element.195), channel_id=1, source_target_pairs={{0,1},{1,0},{2,3},{3,2},{4,5},{5,4},{6,7},{7,6},{8,9},{9,8},{10,11... | collective-permute-start | bytes 3342344 | tf_op jit(solution)/shard_map/ppermute | solution.py:170
  370.4 25.9 %collective-permute-start.27 = (bf16[256,2176]{0,1:T(8,128)(2,1)}, bf16[256,2176]{0,1:T(8,128)(2,1)}, u32[]{:S(2)}, u32[]{:S(2)}) collective-permute-start(bf16[256,2176]{0,1:T(8,128)(2,1)} %get-tuple-element.194), channel_id=1, source_target_pairs={{0,1},{1,0},{2,3},{3,2},{4,5},{5,4},{6,7},{7,6},{8,9},{9,8},{10,11... | collective-permute-start | bytes 3342344 | tf_op jit(solution)/shard_map/ppermute | solution.py:170
  378.3 52.8 %collective-permute-start.30 = (bf16[272,4352]{1,0:T(8,128)(2,1)}, bf16[272,4352]{1,0:T(8,128)(2,1)S(1)}, u32[]{:S(2)}, u32[]{:S(2)}) collective-permute-start(bf16[272,4352]{1,0:T(8,128)(2,1)} %get-tuple-element.128), channel_id=1, source_target_pairs={{0,2},{2,0},{1,3},{3,1},{4,6},{6,4},{5,7},{7,5},{8,10},{10,8},{9,1... | collective-permute-start | bytes 7102472 | tf_op jit(solution)/shard_map/ppermute | solution.py:176
  410.0 24.8 %collective-permute-start.34 = (bf16[136,1088]{1,0:T(8,128)(2,1)}, bf16[136,1088]{1,0:T(8,128)(2,1)S(1)}, u32[]{:S(2)}, u32[]{:S(2)}) collective-permute-start(bf16[136,1088]{1,0:T(8,128)(2,1)} %constant_dynamic-slice_fusion.15), channel_id=1, source_target_pairs={{0,16},{16,0},{8,24},{24,8},{1,17},{17,1},{9,25},{25,9},{2,18},{18... | collective-permute-start | bytes 887816 | tf_op jit(solution)/shard_map/ppermute | solution.py:106
  433.0 25.0 %collective-permute-start.31 = (bf16[256,2176]{0,1:T(8,128)(2,1)}, bf16[256,2176]{0,1:T(8,128)(2,1)}, u32[]{:S(2)}, u32[]{:S(2)}) collective-permute-start(bf16[256,2176]{0,1:T(8,128)(2,1)} %get-tuple-element.132), channel_id=1, source_target_pairs={{0,2},{2,0},{1,3},{3,1},{4,6},{6,4},{5,7},{7,5},{8,10},{10,8},{9,1... | collective-permute-start | bytes 3342344 | tf_op jit(solution)/shard_map/ppermute | solution.py:176
  438.1 45.1 %collective-permute-start.49 = (bf16[136,4352]{1,0:T(8,128)(2,1)}, bf16[136,4352]{1,0:T(8,128)(2,1)}, u32[]{:S(2)}, u32[]{:S(2)}) collective-permute-start(bf16[136,4352]{1,0:T(8,128)(2,1)} %constant_dynamic-slice_fusion.8), channel_id=1, source_target_pairs={{0,4},{4,0},{1,5},{5,1},{2,6},{6,2},{3,7},{7,3},{8,12},{12,8},{9,1... | collective-permute-start | bytes 3551240 | tf_op jit(solution)/shard_map/ppermute | solution.py:106
  465.9 28.5 %collective-permute-start.69 = (bf16[136,1088]{1,0:T(8,128)(2,1)}, bf16[136,1088]{1,0:T(8,128)(2,1)S(1)}, u32[]{:S(2)}, u32[]{:S(2)}) collective-permute-start(bf16[136,1088]{1,0:T(8,128)(2,1)} %add_convert_fusion.28), channel_id=1, source_target_pairs={{0,16},{16,0},{8,24},{24,8},{1,17},{17,1},{9,25},{25,9},{2,18},{18... | collective-permute-start | bytes 887816 | tf_op jit(solution)/shard_map/ppermute | solution.py:112
  470.1 89.9 %collective-permute-start.47 = (bf16[272,2240]{1,0:T(8,128)(2,1)}, bf16[272,2240]{1,0:T(8,128)(2,1)}, u32[]{:S(2)}, u32[]{:S(2)}) collective-permute-start(bf16[272,2240]{1,0:T(8,128)(2,1)} %get-tuple-element.191), channel_id=1, source_target_pairs={{0,1},{1,0},{2,3},{3,2},{4,5},{5,4},{6,7},{7,6},{8,9},{9,8},{10,11... | collective-permute-start | bytes 3655688 | tf_op jit(solution)/shard_map/ppermute | solution.py:170
  470.1 89.9 %collective-permute-start.48 = (bf16[272,2240]{1,0:T(8,128)(2,1)}, bf16[272,2240]{1,0:T(8,128)(2,1)}, u32[]{:S(2)}, u32[]{:S(2)}) collective-permute-start(bf16[272,2240]{1,0:T(8,128)(2,1)} %get-tuple-element.190), channel_id=1, source_target_pairs={{0,1},{1,0},{2,3},{3,2},{4,5},{5,4},{6,7},{7,6},{8,9},{9,8},{10,11... | collective-permute-start | bytes 3655688 | tf_op jit(solution)/shard_map/ppermute | solution.py:170
  481.6 27.6 %collective-permute-start.59 = (bf16[272,1088]{1,0:T(8,128)(2,1)S(1)}, bf16[272,1088]{1,0:T(8,128)(2,1)S(1)}, u32[]{:S(2)}, u32[]{:S(2)}) collective-permute-start(bf16[272,1088]{1,0:T(8,128)(2,1)S(1)} %copy-done.67), channel_id=1, source_target_pairs={{0,2},{2,0},{1,3},{3,1},{4,6},{6,4},{5,7},{7,5},{8,10},{10,8},{9,1... | collective-permute-start | bytes 1775624 | tf_op jit(solution)/shard_map/ppermute | solution.py:176
  518.3 24.6 %collective-permute-start.51 = (bf16[40,4352]{1,0:T(8,128)(2,1)S(1)}, bf16[40,4352]{1,0:T(8,128)(2,1)S(1)}, u32[]{:S(2)}, u32[]{:S(2)}) collective-permute-start(bf16[40,4352]{1,0:T(8,128)(2,1)S(1)} %constant_dynamic-slice_fusion.6), channel_id=1, source_target_pairs={{0,16},{16,0},{8,24},{24,8},{1,17},{17,1},{9,25},{25,9},{2,18},{18... | collective-permute-start | bytes 1044488 | tf_op jit(solution)/shard_map/ppermute | solution.py:106
  529.6 56.1 %collective-permute-start.71 = (bf16[544,1088]{1,0:T(8,128)(2,1)S(1)}, bf16[544,1088]{1,0:T(8,128)(2,1)S(1)}, u32[]{:S(2)}, u32[]{:S(2)}) collective-permute-start(bf16[544,1088]{1,0:T(8,128)(2,1)S(1)} %pad_maximum_fusion.11), channel_id=1, source_target_pairs={{0,4},{4,0},{1,5},{5,1},{2,6},{6,2},{3,7},{7,3},{8,12},{12,8},{9,1... | collective-permute-start | bytes 3551240 | tf_op jit(solution)/shard_map/ppermute | solution.py:112
  615.2 22.7 %collective-permute-start.68 = (bf16[136,4352]{1,0:T(8,128)(2,1)S(1)}, bf16[136,4352]{1,0:T(8,128)(2,1)S(1)}, u32[]{:S(2)}, u32[]{:S(2)}) collective-permute-start(bf16[136,4352]{1,0:T(8,128)(2,1)S(1)} %pad_maximum_fusion.14), channel_id=1, source_target_pairs={{0,4},{4,0},{1,5},{5,1},{2,6},{6,2},{3,7},{7,3},{8,12},{12,8},{9,1... | collective-permute-start | bytes 3551240 | tf_op jit(solution)/shard_map/ppermute | solution.py:112
  (132 other events, 1425.6 us)
Sparse Core Ops, SparseCore 0:
  121.5 38.0 all-gather.2
